TPU v7x, 32 devices: a whole 2x2x4 slice. The times are simulated.
32 devices in a mesh: seq: 8 (over z, x), head: 4 (over y, core).
Axes of the slice: x: 2, y: 2, z: 4, core: 2. Of those that a mesh axis runs over, the one named last changes fastest.
Arguments:
- tokens: bfloat16 [4, 2048, 2048], P(None, 'seq', 'head'), may hold values from -6 to 6
- cotangent: bfloat16 [4, 2048, 2048], P(None, 'seq', 'head'), may hold values from -6 to 6
- norm_gain: float32 [2048], replicated, may hold values from 0.1 to 1.9
- gate_matrix: bfloat16 [2048, 4096], P(None, 'head'), may hold values from -0.125 to 0.125
- value_matrix: bfloat16 [2048, 4096], P(None, 'head'), may hold values from -0.125 to 0.125
- state_matrix: bfloat16 [2048, 256], replicated, may hold values from -0.125 to 0.125
- step_matrix: bfloat16 [2048, 64], P(None, 'head'), may hold values from -0.125 to 0.125
- value_kernel: float32 [4, 4096], P(None, 'head'), may hold values from -3 to 3
- value_bias: float32 [4096], P('head'), may hold values from -3 to 3
- state_kernel: float32 [4, 256], replicated, may hold values from -3 to 3
- state_bias: float32 [256], replicated, may hold values from -3 to 3
- step_bias: float32 [64], P('head'), may hold values from -9 to -2
- log_rate: float32 [64], P('head'), may hold values from -1 to 1.5
- skip_gain: float32 [64], P('head'), may hold values from 0.5 to 1.5
- gate_gain: float32 [4096], P('head'), may hold values from 0.1 to 1.9
- output_matrix: bfloat16 [4096, 2048], P('head'), may hold values from -0.09375 to 0.09375
Outputs:
- layer_out: bfloat16 [4, 2048, 2048], P(None, 'seq', 'head')
- token_grad: float32 [4, 2048, 2048], P(None, 'seq', 'head')
- norm_gain_grad: float32 [2048], P('head')
- gate_matrix_grad: float32 [2048, 4096], P('seq', 'head')
- value_matrix_grad: float32 [2048, 4096], P('seq', 'head')
- state_matrix_grad: float32 [2048, 256], P('head')
- step_matrix_grad: float32 [2048, 64], P('seq', 'head')
- value_kernel_grad: float32 [4, 4096], P(None, 'head')
- value_bias_grad: float32 [4096], P('head')
- state_kernel_grad: float32 [4, 256], replicated
- state_bias_grad: float32 [256], replicated
- step_bias_grad: float32 [64], P('head')
- log_rate_grad: float32 [64], P('head')
- skip_gain_grad: float32 [64], P('head')
- gate_gain_grad: float32 [4096], P('head')
- output_matrix_grad: float32 [4096, 2048], P('head', 'seq')
All inputs are finite; a program needn't handle non-finite values.
Results may differ from a plain program's by a relative error of at most 0.012.
The roundings to bfloat16 on the way count: a program that leaves them out, or rounds other values in their place, can miss the bound.
Values may be sent and summed in bfloat16 or wider, within the bound.
A program may use at most 192 MiB of HBM per device.

v0:
```python
import jax
import jax.numpy as jnp
from jax import lax
from jax.sharding import PartitionSpec as P

HIGH = lax.Precision.HIGHEST
EPSILON = 1e-05


def shifted(block, axis, distance):
    devices = range(lax.axis_size(axis))
    route = [(i - distance, i) for i in devices if i - distance in devices]
    return lax.ppermute(block, axis, route)


def prefix(part, axis, combine, identity, reverse):
    count = lax.axis_size(axis)
    place = lax.axis_index(axis)
    ahead = count - 1 - place if reverse else place
    gathered = jax.tree.map(lambda a: lax.all_gather(a, axis), part)
    state = jax.tree.map(lambda a, e: jnp.zeros_like(a) + jnp.asarray(e, a.dtype), part, identity)

    def one(lap, state):
        source = count - 1 - lap if reverse else lap
        return combine(
            state, jax.tree.map(lambda a: lax.dynamic_index_in_dim(a, source, 0, False), gathered)
        )

    return lax.fori_loop(0, ahead, one, state)


def silu_slope(value):
    sigma = jax.nn.sigmoid(value)
    return sigma * (1.0 + value * (1.0 - sigma))


def carry_state(earlier, later):
    return (earlier[0] * later[0], later[0][..., None, None] * earlier[1] + later[1])


def depthwise(padded, kernel, offset, length):
    summed = offset + kernel[0] * padded[:, 0:length]
    for tap_index in range(1, kernel.shape[0]):
        summed = summed + kernel[tap_index] * padded[:, tap_index : tap_index + length]
    return summed


def depthwise_back(extended, kernel, length):
    margin = kernel.shape[0] - 1
    summed = kernel[0] * extended[:, margin : margin + length]
    for tap_index in range(1, kernel.shape[0]):
        summed = (
            summed
            + kernel[tap_index] * extended[:, margin - tap_index : margin - tap_index + length]
        )
    return summed


def kernel_sums(padded, pre_grad, length, taps):
    return jnp.stack(
        [
            jnp.sum(pre_grad * padded[:, tap_index : tap_index + length], axis=(0, 1))
            for tap_index in range(taps)
        ]
    )


def back_product(grad_rows, matrix):
    return jnp.einsum("rc,dc->rd", grad_rows, matrix, preferred_element_type=jnp.float32)


def row_product(rows_in, grad_rows):
    return jnp.einsum("rd,rc->dc", rows_in, grad_rows, preferred_element_type=jnp.float32)


def local(
    tokens,
    cotangent,
    norm_gain,
    gate_matrix,
    value_matrix,
    state_matrix,
    step_matrix,
    value_kernel,
    value_bias,
    state_kernel,
    state_bias,
    step_bias,
    log_rate,
    skip_gain,
    gate_gain,
    output_matrix,
):
    seq_count, block_len, share = tokens.shape
    width = gate_matrix.shape[0]
    inner_local = gate_matrix.shape[1]
    heads_local = step_bias.shape[0]
    head_width = inner_local // heads_local
    states = state_matrix.shape[1] // 2
    taps = value_kernel.shape[0]
    row_count = seq_count * block_len
    head_count = lax.axis_size("head")
    head_rank = lax.axis_index("head")
    inner_total = inner_local * head_count
    whole_in, whole_cot = (
        lax.all_gather(tokens, "head", axis=2, tiled=True),
        lax.all_gather(cotangent, "head", axis=2, tiled=True),
    )
    plain = whole_in.astype(jnp.float32)
    rstd = lax.rsqrt(jnp.mean(plain * plain, axis=-1, keepdims=True) + EPSILON)
    normal_in = (plain * rstd * norm_gain).astype(jnp.bfloat16)
    flat_in = normal_in.reshape(row_count, width)
    gate_pre = jnp.dot(flat_in, gate_matrix, preferred_element_type=jnp.float32).reshape(
        seq_count, block_len, inner_local
    )
    value_pre = jnp.dot(flat_in, value_matrix, preferred_element_type=jnp.float32).reshape(
        seq_count, block_len, inner_local
    )
    state_pre = jnp.dot(flat_in, state_matrix, preferred_element_type=jnp.float32).reshape(
        seq_count, block_len, 2 * states
    )
    step_pre = jnp.dot(flat_in, step_matrix, preferred_element_type=jnp.float32).reshape(
        seq_count, block_len, heads_local
    )
    cut = block_len - taps + 1
    value_edge, state_edge = shifted((value_pre[:, cut:], state_pre[:, cut:]), "seq", 1)
    value_padded = jnp.concatenate([value_edge, value_pre], axis=1)
    state_padded = jnp.concatenate([state_edge, state_pre], axis=1)
    value_conv = depthwise(value_padded, value_kernel, value_bias, block_len)
    state_conv = depthwise(state_padded, state_kernel, state_bias, block_len)
    values = jax.nn.silu(value_conv).astype(jnp.bfloat16)
    basis = jax.nn.silu(state_conv).astype(jnp.bfloat16)
    in_basis = basis[..., :states]
    out_basis = basis[..., states:]
    step_in = step_pre + step_bias
    step_size = jax.nn.softplus(step_in)
    rate = -jnp.exp(log_rate)
    cumulative = jnp.cumsum(step_size * rate, axis=1)
    final = cumulative[:, -1]
    cum_heads = jnp.transpose(cumulative, (0, 2, 1))
    step_heads = jnp.transpose(step_size, (0, 2, 1))
    lower = lax.broadcasted_iota(jnp.int32, (block_len, block_len), 0) >= lax.broadcasted_iota(
        jnp.int32, (block_len, block_len), 1
    )
    scores = jnp.einsum("stn,srn->str", out_basis, in_basis, preferred_element_type=jnp.float32)
    gap = cum_heads[:, :, :, None] - cum_heads[:, :, None, :]
    decay = jnp.where(lower, jnp.exp(jnp.where(lower, gap, 0.0)), 0.0)
    weights = (scores[:, None] * decay * step_heads[:, :, None, :]).astype(jnp.bfloat16)
    heads_x = values.reshape(seq_count, block_len, heads_local, head_width)
    heads_plain = heads_x.astype(jnp.float32)
    intra = jnp.einsum("shtr,srhp->sthp", weights, heads_x, preferred_element_type=jnp.float32)
    factor = jnp.exp(final[:, None, :] - cumulative) * step_size
    scaled_x = (heads_plain * factor[..., None]).astype(jnp.bfloat16)
    local_state = jnp.einsum(
        "srhp,srn->shpn", scaled_x, in_basis, preferred_element_type=jnp.float32
    )
    block_decay = jnp.exp(final)
    identity = (jnp.ones_like(block_decay), jnp.zeros_like(local_state))
    incoming = prefix((block_decay, local_state), "seq", carry_state, identity, False)[1]
    incoming_low = incoming.astype(jnp.bfloat16)
    inner_v = jnp.einsum(
        "stn,shpn->sthp", out_basis, incoming_low, preferred_element_type=jnp.float32
    )
    growth = jnp.exp(cumulative)[..., None]
    mixed = intra + growth * inner_v + skip_gain[:, None] * heads_plain
    mixed = mixed.reshape(seq_count, block_len, inner_local)
    gate_act = jax.nn.silu(gate_pre)
    gated = mixed * gate_act
    square_sum = lax.psum(jnp.sum(gated * gated, axis=-1), "head")
    grstd = lax.rsqrt(square_sum / inner_total + EPSILON)[..., None]
    normed = (gated * grstd * gate_gain).astype(jnp.bfloat16)
    flat_normed = normed.reshape(row_count, inner_local)
    partial_value = jnp.dot(flat_normed, output_matrix, preferred_element_type=jnp.float32).reshape(
        seq_count, block_len, width
    )
    branch = lax.psum_scatter(partial_value, "head", scatter_dimension=2, tiled=True)
    layer_out = (tokens.astype(jnp.float32) + branch).astype(jnp.bfloat16)
    flat_cot = whole_cot.reshape(row_count, width)
    normed_grad = back_product(flat_cot, output_matrix).reshape(seq_count, block_len, inner_local)
    output_partial = jnp.einsum(
        "ri,rd->id", flat_normed, flat_cot, preferred_element_type=jnp.float32
    )
    gate_gain_part = jnp.sum(normed_grad * gated * grstd, axis=(0, 1))
    gained = normed_grad * gate_gain
    cross_sum = lax.psum(jnp.sum(gained * gated, axis=-1), "head")
    gated_grad = (
        grstd * gained - gated * (grstd * grstd * grstd) * (cross_sum / inner_total)[..., None]
    )
    mixed_grad = (gated_grad * gate_act).astype(jnp.bfloat16)
    gate_grad_low = (gated_grad * mixed * silu_slope(gate_pre)).astype(jnp.bfloat16)
    dy_heads = mixed_grad.reshape(seq_count, block_len, heads_local, head_width)
    dy_plain = dy_heads.astype(jnp.float32)
    weight_grad = jnp.einsum(
        "sthp,srhp->shtr", dy_heads, heads_x, preferred_element_type=jnp.float32
    )
    through = weight_grad * decay
    score_grad = jnp.sum(through * step_heads[:, :, None, :], axis=1)
    with_scores = through * scores[:, None]
    log_part = with_scores * step_heads[:, :, None, :]
    step_from_weights = jnp.sum(with_scores, axis=2)
    cum_grad = jnp.sum(log_part, axis=3) - jnp.sum(log_part, axis=2)
    x_grad = jnp.einsum("shtr,sthp->srhp", weights, dy_heads, preferred_element_type=jnp.float32)
    v_grad = (dy_plain * growth).astype(jnp.bfloat16)
    inter_cum = jnp.sum(dy_plain * growth * inner_v, axis=3)
    incoming_grad = jnp.einsum(
        "sthp,stn->shpn", v_grad, out_basis, preferred_element_type=jnp.float32
    )
    out_basis_grad = jnp.einsum(
        "sthp,shpn->stn", v_grad, incoming_low, preferred_element_type=jnp.float32
    )
    chain_grad = prefix((block_decay, incoming_grad), "seq", carry_state, identity, True)[1]
    total_grad = block_decay * jnp.sum(chain_grad * incoming, axis=(2, 3))
    chain_low = chain_grad.astype(jnp.bfloat16)
    scaled_grad = jnp.einsum(
        "shpn,srn->srhp", chain_low, in_basis, preferred_element_type=jnp.float32
    )
    in_basis_grad = jnp.einsum(
        "shpn,srhp->srn", chain_low, scaled_x, preferred_element_type=jnp.float32
    )
    factor_grad = jnp.sum(scaled_grad * heads_plain, axis=3)
    x_grad = x_grad + scaled_grad * factor[..., None] + skip_gain[:, None] * dy_plain
    skip_part = jnp.sum(dy_plain * heads_plain, axis=(0, 1, 3))
    via_factor = factor_grad * factor
    total_grad = total_grad + jnp.sum(via_factor, axis=1)
    last_token = lax.broadcasted_iota(jnp.int32, (1, block_len, 1), 1) == block_len - 1
    cum_tokens = jnp.transpose(cum_grad, (0, 2, 1)) + inter_cum - via_factor
    cum_tokens = cum_tokens + jnp.where(last_token, total_grad[:, None, :], 0.0)
    rate_grad_tok = jnp.flip(jnp.cumsum(jnp.flip(cum_tokens, 1), axis=1), 1)
    step_grad = (
        jnp.transpose(step_from_weights, (0, 2, 1))
        + factor_grad * jnp.exp(final[:, None, :] - cumulative)
        + rate_grad_tok * rate
    )
    log_rate_part = jnp.sum(rate_grad_tok * step_size, axis=(0, 1)) * rate
    pre_step_grad = step_grad * jax.nn.sigmoid(step_in)
    step_bias_part = jnp.sum(pre_step_grad, axis=(0, 1))
    step_low_flat = pre_step_grad.astype(jnp.bfloat16).reshape(row_count, heads_local)
    out_basis_grad = out_basis_grad + jnp.einsum(
        "str,srn->stn", score_grad, in_basis.astype(jnp.float32), precision=HIGH
    )
    in_basis_grad = in_basis_grad + jnp.einsum(
        "str,stn->srn", score_grad, out_basis.astype(jnp.float32), precision=HIGH
    )
    basis_grad = lax.psum(jnp.concatenate([in_basis_grad, out_basis_grad], axis=-1), "head")
    value_pre_grad = x_grad.reshape(seq_count, block_len, inner_local) * silu_slope(value_conv)
    state_pre_grad = basis_grad * silu_slope(state_conv)
    value_next, state_next = shifted(
        (value_pre_grad[:, : taps - 1], state_pre_grad[:, : taps - 1]), "seq", -1
    )
    value_extended = jnp.concatenate([value_pre_grad, value_next], axis=1)
    state_extended = jnp.concatenate([state_pre_grad, state_next], axis=1)
    value_low_flat = (
        depthwise_back(value_extended, value_kernel, block_len)
        .astype(jnp.bfloat16)
        .reshape(row_count, inner_local)
    )
    state_low_flat = (
        depthwise_back(state_extended, state_kernel, block_len)
        .astype(jnp.bfloat16)
        .reshape(row_count, 2 * states)
    )
    value_kernel_part = kernel_sums(value_padded, value_pre_grad, block_len, taps)
    value_bias_part = jnp.sum(value_pre_grad, axis=(0, 1))
    state_kernel_part = kernel_sums(state_padded, state_pre_grad, block_len, taps)
    state_bias_part = jnp.sum(state_pre_grad, axis=(0, 1))
    gate_low_flat = gate_grad_low.reshape(row_count, inner_local)
    column_share = 2 * states // head_count
    state_columns = lax.dynamic_slice_in_dim(
        state_low_flat, head_rank * column_share, column_share, 1
    )
    matrix_columns = lax.dynamic_slice_in_dim(
        state_matrix, head_rank * column_share, column_share, 1
    )
    normal_partial = back_product(gate_low_flat, gate_matrix) + back_product(
        value_low_flat, value_matrix
    )
    normal_partial = (
        normal_partial
        + back_product(state_columns, matrix_columns)
        + back_product(step_low_flat, step_matrix)
    )
    normal_partial = normal_partial.reshape(seq_count, block_len, width)
    gain_share = lax.dynamic_slice_in_dim(norm_gain, head_rank * share, share, 0)
    own_hat = tokens.astype(jnp.float32) * rstd
    normal_grad = lax.psum_scatter(normal_partial, "head", scatter_dimension=2, tiled=True)
    row_total = lax.psum(
        jnp.sum(normal_grad * gain_share * own_hat, axis=-1, keepdims=True), "head"
    )
    token_grad = cotangent.astype(jnp.float32) + rstd * (
        normal_grad * gain_share - own_hat * row_total / width
    )
    norm_gain_part = jnp.sum(normal_grad * own_hat, axis=(0, 1))
    gate_partial = row_product(flat_in, gate_low_flat)
    value_partial = row_product(flat_in, value_low_flat)
    step_partial = row_product(flat_in, step_low_flat)
    own_rows = lax.dynamic_slice_in_dim(normal_in, head_rank * share, share, 2).reshape(
        row_count, share
    )
    state_partial = row_product(own_rows, state_low_flat)
    gate_matrix_grad, value_matrix_grad, step_matrix_grad, output_matrix_grad = (
        lax.psum_scatter(gate_partial, "seq", scatter_dimension=0, tiled=True),
        lax.psum_scatter(value_partial, "seq", scatter_dimension=0, tiled=True),
        lax.psum_scatter(step_partial, "seq", scatter_dimension=0, tiled=True),
        lax.psum_scatter(output_partial, "seq", scatter_dimension=1, tiled=True),
    )
    summed = lax.psum(
        (
            state_partial,
            norm_gain_part,
            value_kernel_part,
            value_bias_part,
            state_kernel_part,
            state_bias_part,
            step_bias_part,
            log_rate_part,
            skip_part,
            gate_gain_part,
        ),
        "seq",
    )
    return (
        layer_out,
        token_grad,
        summed[1],
        gate_matrix_grad,
        value_matrix_grad,
        summed[0],
        step_matrix_grad,
        summed[2],
        summed[3],
        summed[4],
        summed[5],
        summed[6],
        summed[7],
        summed[8],
        summed[9],
        output_matrix_grad,
    )


def solution(mesh):
    in_specs = (
        P(None, "seq", "head"),
        P(None, "seq", "head"),
        P(),
        P(None, "head"),
        P(None, "head"),
        P(),
        P(None, "head"),
        P(None, "head"),
        P("head"),
        P(),
        P(),
        P("head"),
        P("head"),
        P("head"),
        P("head"),
        P("head", None),
    )
    out_specs = (
        P(None, "seq", "head"),
        P(None, "seq", "head"),
        P("head"),
        P("seq", "head"),
        P("seq", "head"),
        P("head", None),
        P("seq", "head"),
        P(None, "head"),
        P("head"),
        P(),
        P(),
        P("head"),
        P("head"),
        P("head"),
        P("head"),
        P("head", "seq"),
    )
    return jax.shard_map(local, mesh=mesh, in_specs=in_specs, out_specs=out_specs, check_vma=False)
```

profile of v0, /device:TPU:0, one launch (start us, length us, event | category | flops | bytes accessed | tf_op | source)
XLA Modules:
  0.0 1523.4 jit_solution(14985782426660822463)
XLA Ops:
  12.1 35.3 %all-gather.8.cloned.1.call-done = bf16[4,256,2048]{1,2,0:T(8,128)(2,1)} async-done(((bf16[4,256,512]{1,2,0:T(8,128)(2,1)}), bf16[4,256,2048]{1,2,0:T(8,128)(2,1)}) %all-gather.8.cloned.1.call-update) | async-done | bytes 4194320 | tf_op jit(solution)/shard_map/all_gather | solution.py:106
  67.3 10.2 fusion.30
  108.9 27.1 %all-gather = f32[32,1,16]{2,1,0:T(1,128)S(1)} all-gather(f32[4,1,16]{2,1,0:T(1,128)S(1)} %bitcast.242), channel_id=2, replica_groups=mesh['seq'=8,'head'=4] {'seq'}, dimensions={0}, use_global_device_ids=true | all-gather | bytes 2304 | tf_op jit(solution)/shard_map/all_gather | solution.py:20
  138.2 192.5 %all-gather.12.cloned.1.call-done = f32[32,16,64,128]{3,2,1,0:T(8,128)} async-done(((f32[4,16,64,128]{3,2,1,0:T(8,128)}), f32[32,16,64,128]{3,2,1,0:T(8,128)}) %all-gather.12.cloned.1.call-update) | async-done | bytes 16777232 | tf_op jit(solution)/shard_map/all_gather | solution.py:20
  345.5 13.2 multiply_reduce_fusion.11
  358.7 18.4 %psum.98 = f32[4,256]{1,0:T(4,128)S(1)} all-reduce(f32[4,256]{1,0:T(4,128)S(1)} %get-tuple-element.199), channel_id=1, replica_groups=mesh['seq'=8,'head'=4] {'head'}, use_global_device_ids=true, to_apply=%region_6.7 | all-reduce | flops 1024 | bytes 8192 | tf_op jit(solution)/shard_map/psum | solution.py:169
  377.2 11.9 multiply_reduce_fusion.4
  395.0 10.3 multiply_reduce_fusion.5
  417.9 13.3 multiply_reduce_fusion.1
  449.4 203.2 %all-gather.14.cloned.1.call-done = f32[32,16,64,128]{3,2,1,0:T(8,128)} async-done(((f32[4,16,64,128]{3,2,1,0:T(8,128)}), f32[32,16,64,128]{3,2,1,0:T(8,128)}) %all-gather.14.cloned.1.call-update) | async-done | bytes 16777232 | tf_op jit(solution)/shard_map/all_gather | solution.py:20
  654.3 26.7 %while.27 = (s32[]{:T(128)}, f32[4,16,64,128]{3,2,1,0:T(8,128)}, s32[]{:T(128)}, f32[8,4,16]{2,1,0:T(4,128)S(1)}, f32[8,4,16,64,128]{4,3,2,1,0:T(8,128)}, /*index=5*/s32[]{:T(128)}, s32[]{:T(128)}, s32[]{:T(128)}, s32[]{:T(128)}) while((s32[]{:T(128)}, f32[4,16,64,128]{3,2,1,0:T(8,128)}, s32[]{:T(128)}, f32[8,4,16]{2,1,0:T(4,128)S(1)}, ...), condition=%wide.region_11.12_spmd, body=%wide.region_10.11_spmd.sunk | while | flops 1048582 | bytes 6292379 | solution.py:29
  718.2 10.9 multiply_reduce_fusion.9
  769.9 12.9 fusion.26
  783.1 12.0 convolution_bitcast_fusion
  795.2 10.6 convolution_bitcast_fusion.2
  812.9 10.7 convolution_bitcast_fusion.1
  825.0 16.1 %reduce-scatter.9.cloned.1.call-done = f32[4,256,512]{2,1,0:T(8,128)} async-done(((f32[4,256,2048]{2,1,0:T(8,128)}), f32[4,256,512]{2,1,0:T(8,128)}) %reduce-scatter.9.cloned.1.call-update) | async-done | bytes 2097168 | tf_op jit(solution)/shard_map/reduce_scatter | solution.py:285
  843.4 38.1 %all-reduce = (f32[512]{0:T(512)}, f32[4,1024]{1,0:T(4,128)}, f32[1024]{0:T(1024)}, f32[4,256]{1,0:T(4,128)}, f32[256]{0:T(256)}, /*index=5*/f32[16]{0:T(128)}, f32[16]{0:T(128)}, f32[16]{0:T(128)}, f32[1024]{0:T(1024)}) all-reduce(f32[512]{0:T(512)S(1)} %get-tuple-element.157, ...), channel_id=1, replica_groups=mesh['seq'=8,'head'=4] {'seq'}, use_global_device_ids=true, to_apply=%region_27.28 | all-reduce | flops 7984 | bytes 63872 | tf_op jit(solution)/shard_map/psum | solution.py:306
  887.6 28.0 %reduce-scatter.7.cloned.1.call-done = f32[4,256,512]{2,1,0:T(8,128)} async-done(((f32[4,256,2048]{2,1,0:T(8,128)}), f32[4,256,512]{2,1,0:T(8,128)}) %reduce-scatter.7.cloned.1.call-update) | async-done | bytes 2097168 | tf_op jit(solution)/shard_map/reduce_scatter | solution.py:176
  920.2 149.4 %reduce-scatter.17.cloned.1.call-done = f32[1024,256]{1,0:T(8,128)} async-done(((f32[1024,2048]{1,0:T(8,128)}), f32[1024,256]{1,0:T(8,128)}) %reduce-scatter.17.cloned.1.call-update) | async-done | bytes 1048592 | tf_op jit(solution)/shard_map/reduce_scatter | solution.py:304
  1069.7 152.3 %reduce-scatter.11.cloned.1.call-done = f32[256,1024]{1,0:T(8,128)} async-done(((f32[2048,1024]{1,0:T(8,128)}), f32[256,1024]{1,0:T(8,128)}) %reduce-scatter.11.cloned.1.call-update) | async-done | bytes 1048592 | tf_op jit(solution)/shard_map/reduce_scatter | solution.py:301
  1221.9 64.4 %reduce-scatter.15.cloned.1.call-done = f32[256,16]{0,1:T(8,128)} async-done(((f32[2048,16]{0,1:T(8,128)}), f32[256,16]{0,1:T(8,128)}) %reduce-scatter.15.cloned.1.call-update) | async-done | bytes 16400 | tf_op jit(solution)/shard_map/reduce_scatter | solution.py:303
  1286.3 75.8 %all-reduce.6.cloned.1.call-done = f32[512,256]{1,0:T(8,128)} async-done(((f32[512,256]{1,0:T(8,128)}), f32[512,256]{1,0:T(8,128)}) %all-reduce.6.cloned.1.call-update) | async-done | bytes 524304 | tf_op jit(solution)/shard_map/psum | solution.py:306
  1362.1 152.4 %reduce-scatter.13.cloned.1.call-done = f32[256,1024]{1,0:T(8,128)} async-done(((f32[2048,1024]{1,0:T(8,128)}), f32[256,1024]{1,0:T(8,128)}) %reduce-scatter.13.cloned.1.call-update) | async-done | bytes 1048592 | tf_op jit(solution)/shard_map/reduce_scatter | solution.py:302
  (289 shorter events, 238.9 us)
Async XLA Ops:
  7.2 40.2 %all-gather.8.cloned.1.call-start = ((), (), s32[]{:S(2)}) async-start(), calls=%async_computation.6 | async-start | bytes 5242880 | tf_op jit(solution)/shard_map/all_gather | solution.py:106
  9.6 321.1 %all-gather.12.cloned.1.call-start = ((), (), s32[]{:S(2)}) async-start(), calls=%async_computation.16 | async-start | bytes 18874368 | tf_op jit(solution)/shard_map/all_gather | solution.py:20
  11.2 72.8 %copy-start.50 = (f32[1,256]{1,0:T(1,128)}, f32[1,256]{1,0:T(1,128)S(1)}, u32[]{:S(2)}) copy-start(f32[1,256]{1,0:T(1,128)S(1)} %get-tuple-element.221) | copy-start | bytes 3076
  11.2 72.8 %copy-start.52 = (f32[1,256]{1,0:T(1,128)}, f32[1,256]{1,0:T(1,128)S(1)}, u32[]{:S(2)}) copy-start(f32[1,256]{1,0:T(1,128)S(1)} %get-tuple-element.222) | copy-start | bytes 3076
  11.2 72.8 %copy-start.54 = (f32[1,256]{1,0:T(1,128)}, f32[1,256]{1,0:T(1,128)S(1)}, u32[]{:S(2)}) copy-start(f32[1,256]{1,0:T(1,128)S(1)} %get-tuple-element.223) | copy-start | bytes 3076
  11.2 72.8 %copy-start.56 = (f32[1,256]{1,0:T(1,128)}, f32[1,256]{1,0:T(1,128)S(1)}, u32[]{:S(2)}) copy-start(f32[1,256]{1,0:T(1,128)S(1)} %get-tuple-element.224) | copy-start | bytes 3076
  12.1 76.3 %copy-start.39 = (f32[1,1024]{1,0:T(1,128)}, f32[1,1024]{1,0:T(1,128)S(1)}, u32[]{:S(2)}) copy-start(f32[1,1024]{1,0:T(1,128)S(1)} %get-tuple-element.217) | copy-start | bytes 12292
  12.1 76.3 %copy-start.40 = (f32[1,1024]{1,0:T(1,128)}, f32[1,1024]{1,0:T(1,128)S(1)}, u32[]{:S(2)}) copy-start(f32[1,1024]{1,0:T(1,128)S(1)} %get-tuple-element.218) | copy-start | bytes 12292
  59.4 24.5 %collective-permute-start.1 = (f32[4,3,256]{2,1,0:T(4,128)S(1)}, f32[4,3,256]{2,1,0:T(4,128)S(1)}, u32[]{:S(2)}, u32[]{:S(2)}) collective-permute-start(f32[4,3,256]{2,1,0:T(4,128)S(1)} %slice.143), channel_id=1, source_target_pairs={{0,4},{4,8},{8,12},{12,16},{16,20},{20,24},{24,28},{1,5},{5,9},{9,... | collective-permute-start | bytes 36872 | tf_op jit(solution)/shard_map/ppermute | solution.py:13
  80.2 8.2 collective-permute-start
  103.8 273.4 %all-gather.10.cloned.1.call-start = ((), (), s32[]{:S(2)}) async-start(), calls=%async_computation.8 | async-start | bytes 5242880 | tf_op jit(solution)/shard_map/all_gather | solution.py:107
  104.5 548.2 %all-gather.14.cloned.1.call-start = ((), (), s32[]{:S(2)}) async-start(), calls=%async_computation.17 | async-start | bytes 18874368 | tf_op jit(solution)/shard_map/all_gather | solution.py:20
  107.6 225.2 %copy-start.37 = (f32[4,16,256]{2,1,0:T(8,128)}, f32[4,16,256]{2,1,0:T(8,128)S(1)}, u32[]{:S(2)}) copy-start(f32[4,16,256]{2,1,0:T(8,128)S(1)} %copy.197) | copy-start | bytes 196612
  412.9 333.6 %all-reduce.4.cloned.1.call-start = ((), (), s32[]{:S(2)}) async-start(), calls=%async_computation.9 | async-start | bytes 2097152 | tf_op jit(solution)/shard_map/psum | solution.py:244
  689.6 151.5 %reduce-scatter.9.cloned.1.call-start = ((), (), s32[]{:S(2)}) async-start(), calls=%async_computation.10 | async-start | bytes 10485760 | tf_op jit(solution)/shard_map/reduce_scatter | solution.py:285
  731.8 6.4 collective-permute-start.2
  748.8 10.8 collective-permute-start.3
  769.9 145.7 %reduce-scatter.7.cloned.1.call-start = ((), (), s32[]{:S(2)}) async-start(), calls=%async_computation.7 | async-start | bytes 10485760 | tf_op jit(solution)/shard_map/reduce_scatter | solution.py:176
  782.9 286.8 %reduce-scatter.17.cloned.1.call-start = ((), (), s32[]{:S(2)}) async-start(), calls=%async_computation.15 | async-start | bytes 9437184 | tf_op jit(solution)/shard_map/reduce_scatter | solution.py:304
  795.1 426.8 %reduce-scatter.11.cloned.1.call-start = ((), (), s32[]{:S(2)}) async-start(), calls=%async_computation.11 | async-start | bytes 9437184 | tf_op jit(solution)/shard_map/reduce_scatter | solution.py:301
  805.8 480.4 %reduce-scatter.15.cloned.1.call-start = ((), (), s32[]{:S(2)}) async-start(), calls=%async_computation.14 | async-start | bytes 147456 | tf_op jit(solution)/shard_map/reduce_scatter | solution.py:303
  810.1 552.0 %all-reduce.6.cloned.1.call-start = ((), (), s32[]{:S(2)}) async-start(), calls=%async_computation.13 | async-start | bytes 1048576 | tf_op jit(solution)/shard_map/psum | solution.py:306
  812.7 701.8 %reduce-scatter.13.cloned.1.call-start = ((), (), s32[]{:S(2)}) async-start(), calls=%async_computation.12 | async-start | bytes 9437184 | tf_op jit(solution)/shard_map/reduce_scatter | solution.py:302
  823.7 91.9 %copy-start.21 = (bf16[4,256,512]{2,1,0:T(8,128)(2,1)S(1)}, bf16[4,256,512]{2,1,0:T(8,128)(2,1)}, u32[]{:S(2)}) copy-start(bf16[4,256,512]{2,1,0:T(8,128)(2,1)} %param.21) | copy-start | bytes 3145732
  (63 other events, 676.0 us)
Sparse Core Ops, SparseCore 0:
  10.2 37.1 all-gather.7
  103.9 226.7 all-gather.11
  332.3 32.7 all-gather.9
  413.0 239.6 all-gather.13
  689.7 33.3 all-reduce.3
  770.0 71.0 reduce-scatter.8
  843.7 71.8 reduce-scatter.6
  920.2 149.3 reduce-scatter.16
  1073.9 148.0 reduce-scatter.10
  1226.0 60.2 reduce-scatter.14
  1290.7 71.3 all-reduce.5
  1366.1 148.3 reduce-scatter.12
where the time goes:
time: 1530 us; the launch traced here: 1520 us
  waiting for transfers between devices  1070 us (70%)
  matrix products  171 us (11%)
  other arithmetic  107 us (7%)
  blocking collectives  95.6 us (6%)
  local copies, waits for them, and re-layouts  50.3 us (3%)
  between operations  15.5 us (1%)
    all_gather x2, waiting for transfers between devices, prefix(): gathered = jax.tree.map(lambda a: lax.all_gather(a, axis), part)  396 us
    reduce_scatter x1, waiting for transfers between devices, local(): lax.psum_scatter(value_partial, 'seq', scatter_dimension=0, tiled=True)  152 us
    reduce_scatter x1, waiting for transfers between devices, local(): lax.psum_scatter(gate_partial, 'seq', scatter_dimension=0, tiled=True)  152 us
    reduce_scatter x1, waiting for transfers between devices, local(): lax.psum_scatter(output_partial, 'seq', scatter_dimension=1, tiled=True)  149 us
    psum x1, waiting for transfers between devices, local(): lax.psum((state_partial, norm_gain_part, value_kernel_part, value_bias_pa...  75.8 us
    reduce_scatter x1, waiting for transfers between devices, local(): lax.psum_scatter(step_partial, 'seq', scatter_dimension=0, tiled=True)  64.4 us
    dot_general x5, matrix products, back_product(): jnp.einsum('rc,dc->rd', grad_rows, matrix, preferred_element_type=jnp.flo...  39.6 us
    psum x1, blocking collectives, local(): lax.psum((state_partial, norm_gain_part, value_kernel_part, value_bias_pa...  38.1 us
  transfers between devices with their start and end apart: 16, of which 11 were waited for; matrix products, arithmetic and copies ran while one was open for 14% of the time, Pallas kernels for 0%

commit v1 on v0

--- a/solution.py
+++ b/solution.py
@@ -13,29 +13,24 @@
     return lax.ppermute(block, axis, route)
 
 
-def prefix(part, axis, combine, identity, reverse):
-    count = lax.axis_size(axis)
-    place = lax.axis_index(axis)
-    ahead = count - 1 - place if reverse else place
-    gathered = jax.tree.map(lambda a: lax.all_gather(a, axis), part)
-    state = jax.tree.map(lambda a, e: jnp.zeros_like(a) + jnp.asarray(e, a.dtype), part, identity)
-
-    def one(lap, state):
-        source = count - 1 - lap if reverse else lap
-        return combine(
-            state, jax.tree.map(lambda a: lax.dynamic_index_in_dim(a, source, 0, False), gathered)
-        )
-
-    return lax.fori_loop(0, ahead, one, state)
+def regroup(block):
+    members = block.shape[0]
+    count = lax.axis_size("seq")
+    groups = [list(range(i, i + members)) for i in range(0, count, members)]
+    return lax.all_to_all(block, "seq", 0, 0, axis_index_groups=groups, tiled=True)
+
+
+def carried(part, decay, hops, distance):
+    carry = jnp.zeros_like(part)
+    for _ in range(hops):
+        leaving = (decay[..., None, None] * carry + part).astype(jnp.bfloat16)
+        carry = shifted(leaving, "seq", distance).astype(jnp.float32)
+    return carry
 
 
 def silu_slope(value):
     sigma = jax.nn.sigmoid(value)
     return sigma * (1.0 + value * (1.0 - sigma))
-
-
-def carry_state(earlier, later):
-    return (earlier[0] * later[0], later[0][..., None, None] * earlier[1] + later[1])
 
 
 def depthwise(padded, kernel, offset, length):
@@ -71,6 +66,11 @@
 
 def row_product(rows_in, grad_rows):
     return jnp.einsum("rd,rc->dc", rows_in, grad_rows, preferred_element_type=jnp.float32)
+
+
+def summed_low(part, dim):
+    low = part.astype(jnp.bfloat16)
+    return lax.psum_scatter(low, "seq", scatter_dimension=dim, tiled=True).astype(jnp.float32)
 
 
 def local(
@@ -92,6 +92,7 @@
     output_matrix,
 ):
     seq_count, block_len, share = tokens.shape
+    chain = lax.axis_size("seq") // seq_count
     width = gate_matrix.shape[0]
     inner_local = gate_matrix.shape[1]
     heads_local = step_bias.shape[0]
@@ -103,8 +104,8 @@
     head_rank = lax.axis_index("head")
     inner_total = inner_local * head_count
     whole_in, whole_cot = (
-        lax.all_gather(tokens, "head", axis=2, tiled=True),
-        lax.all_gather(cotangent, "head", axis=2, tiled=True),
+        lax.all_gather(regroup(tokens), "head", axis=2, tiled=True),
+        lax.all_gather(regroup(cotangent), "head", axis=2, tiled=True),
     )
     plain = whole_in.astype(jnp.float32)
     rstd = lax.rsqrt(jnp.mean(plain * plain, axis=-1, keepdims=True) + EPSILON)
@@ -122,12 +123,18 @@
     step_pre = jnp.dot(flat_in, step_matrix, preferred_element_type=jnp.float32).reshape(
         seq_count, block_len, heads_local
     )
-    cut = block_len - taps + 1
-    value_edge, state_edge = shifted((value_pre[:, cut:], state_pre[:, cut:]), "seq", 1)
-    value_padded = jnp.concatenate([value_edge, value_pre], axis=1)
-    state_padded = jnp.concatenate([state_edge, state_pre], axis=1)
-    value_conv = depthwise(value_padded, value_kernel, value_bias, block_len)
-    state_conv = depthwise(state_padded, state_kernel, state_bias, block_len)
+    value_flat = value_pre.reshape(1, row_count, inner_local)
+    state_flat = state_pre.reshape(1, row_count, 2 * states)
+    cut = row_count - taps + 1
+    value_edge, state_edge = shifted((value_flat[:, cut:], state_flat[:, cut:]), "seq", seq_count)
+    value_padded = jnp.concatenate([value_edge, value_flat], axis=1)
+    state_padded = jnp.concatenate([state_edge, state_flat], axis=1)
+    value_conv = depthwise(value_padded, value_kernel, value_bias, row_count).reshape(
+        seq_count, block_len, inner_local
+    )
+    state_conv = depthwise(state_padded, state_kernel, state_bias, row_count).reshape(
+        seq_count, block_len, 2 * states
+    )
     values = jax.nn.silu(value_conv).astype(jnp.bfloat16)
     basis = jax.nn.silu(state_conv).astype(jnp.bfloat16)
     in_basis = basis[..., :states]
@@ -155,8 +162,14 @@
         "srhp,srn->shpn", scaled_x, in_basis, preferred_element_type=jnp.float32
     )
     block_decay = jnp.exp(final)
-    identity = (jnp.ones_like(block_decay), jnp.zeros_like(local_state))
-    incoming = prefix((block_decay, local_state), "seq", carry_state, identity, False)[1]
+    whole_decay = jnp.exp(jnp.sum(final, axis=0))
+    ending = local_state[0]
+    for i in range(1, seq_count):
+        ending = block_decay[i][:, None, None] * ending + local_state[i]
+    entering = [carried(ending, whole_decay, chain - 1, seq_count)]
+    for i in range(seq_count - 1):
+        entering.append(block_decay[i][:, None, None] * entering[i] + local_state[i])
+    incoming = jnp.stack(entering)
     incoming_low = incoming.astype(jnp.bfloat16)
     inner_v = jnp.einsum(
         "stn,shpn->sthp", out_basis, incoming_low, preferred_element_type=jnp.float32
@@ -166,23 +179,28 @@
     mixed = mixed.reshape(seq_count, block_len, inner_local)
     gate_act = jax.nn.silu(gate_pre)
     gated = mixed * gate_act
-    square_sum = lax.psum(jnp.sum(gated * gated, axis=-1), "head")
+    flat_cot = whole_cot.reshape(row_count, width)
+    normed_grad = back_product(flat_cot, output_matrix).reshape(seq_count, block_len, inner_local)
+    gained = normed_grad * gate_gain
+    square_sum, cross_sum = lax.psum(
+        jnp.stack([jnp.sum(gated * gated, axis=-1), jnp.sum(gained * gated, axis=-1)]), "head"
+    )
     grstd = lax.rsqrt(square_sum / inner_total + EPSILON)[..., None]
     normed = (gated * grstd * gate_gain).astype(jnp.bfloat16)
     flat_normed = normed.reshape(row_count, inner_local)
     partial_value = jnp.dot(flat_normed, output_matrix, preferred_element_type=jnp.float32).reshape(
         seq_count, block_len, width
     )
-    branch = lax.psum_scatter(partial_value, "head", scatter_dimension=2, tiled=True)
-    layer_out = (tokens.astype(jnp.float32) + branch).astype(jnp.bfloat16)
-    flat_cot = whole_cot.reshape(row_count, width)
-    normed_grad = back_product(flat_cot, output_matrix).reshape(seq_count, block_len, inner_local)
+    branch = lax.psum_scatter(
+        partial_value.astype(jnp.bfloat16), "head", scatter_dimension=2, tiled=True
+    )
+    layer_out = (tokens.astype(jnp.float32) + regroup(branch).astype(jnp.float32)).astype(
+        jnp.bfloat16
+    )
     output_partial = jnp.einsum(
         "ri,rd->id", flat_normed, flat_cot, preferred_element_type=jnp.float32
     )
     gate_gain_part = jnp.sum(normed_grad * gated * grstd, axis=(0, 1))
-    gained = normed_grad * gate_gain
-    cross_sum = lax.psum(jnp.sum(gained * gated, axis=-1), "head")
     gated_grad = (
         grstd * gained - gated * (grstd * grstd * grstd) * (cross_sum / inner_total)[..., None]
     )
@@ -208,7 +226,13 @@
     out_basis_grad = jnp.einsum(
         "sthp,shpn->stn", v_grad, incoming_low, preferred_element_type=jnp.float32
     )
-    chain_grad = prefix((block_decay, incoming_grad), "seq", carry_state, identity, True)[1]
+    starting = incoming_grad[-1]
+    for i in range(seq_count - 2, -1, -1):
+        starting = block_decay[i][:, None, None] * starting + incoming_grad[i]
+    returning = [carried(starting, whole_decay, chain - 1, -seq_count)]
+    for i in range(seq_count - 1, 0, -1):
+        returning.insert(0, block_decay[i][:, None, None] * returning[0] + incoming_grad[i])
+    chain_grad = jnp.stack(returning)
     total_grad = block_decay * jnp.sum(chain_grad * incoming, axis=(2, 3))
     chain_low = chain_grad.astype(jnp.bfloat16)
     scaled_grad = jnp.einsum(
@@ -242,26 +266,28 @@
         "str,stn->srn", score_grad, out_basis.astype(jnp.float32), precision=HIGH
     )
     basis_grad = lax.psum(jnp.concatenate([in_basis_grad, out_basis_grad], axis=-1), "head")
-    value_pre_grad = x_grad.reshape(seq_count, block_len, inner_local) * silu_slope(value_conv)
-    state_pre_grad = basis_grad * silu_slope(state_conv)
+    value_pre_grad = x_grad.reshape(1, row_count, inner_local) * silu_slope(value_conv).reshape(
+        1, row_count, inner_local
+    )
+    state_pre_grad = (basis_grad * silu_slope(state_conv)).reshape(1, row_count, 2 * states)
     value_next, state_next = shifted(
-        (value_pre_grad[:, : taps - 1], state_pre_grad[:, : taps - 1]), "seq", -1
+        (value_pre_grad[:, : taps - 1], state_pre_grad[:, : taps - 1]), "seq", -seq_count
     )
     value_extended = jnp.concatenate([value_pre_grad, value_next], axis=1)
     state_extended = jnp.concatenate([state_pre_grad, state_next], axis=1)
     value_low_flat = (
-        depthwise_back(value_extended, value_kernel, block_len)
+        depthwise_back(value_extended, value_kernel, row_count)
         .astype(jnp.bfloat16)
         .reshape(row_count, inner_local)
     )
     state_low_flat = (
-        depthwise_back(state_extended, state_kernel, block_len)
+        depthwise_back(state_extended, state_kernel, row_count)
         .astype(jnp.bfloat16)
         .reshape(row_count, 2 * states)
     )
-    value_kernel_part = kernel_sums(value_padded, value_pre_grad, block_len, taps)
+    value_kernel_part = kernel_sums(value_padded, value_pre_grad, row_count, taps)
     value_bias_part = jnp.sum(value_pre_grad, axis=(0, 1))
-    state_kernel_part = kernel_sums(state_padded, state_pre_grad, block_len, taps)
+    state_kernel_part = kernel_sums(state_padded, state_pre_grad, row_count, taps)
     state_bias_part = jnp.sum(state_pre_grad, axis=(0, 1))
     gate_low_flat = gate_grad_low.reshape(row_count, inner_local)
     column_share = 2 * states // head_count
@@ -281,13 +307,16 @@
     )
     normal_partial = normal_partial.reshape(seq_count, block_len, width)
     gain_share = lax.dynamic_slice_in_dim(norm_gain, head_rank * share, share, 0)
-    own_hat = tokens.astype(jnp.float32) * rstd
-    normal_grad = lax.psum_scatter(normal_partial, "head", scatter_dimension=2, tiled=True)
+    own_hat = lax.dynamic_slice_in_dim(plain, head_rank * share, share, 2) * rstd
     row_total = lax.psum(
-        jnp.sum(normal_grad * gain_share * own_hat, axis=-1, keepdims=True), "head"
-    )
-    token_grad = cotangent.astype(jnp.float32) + rstd * (
-        normal_grad * gain_share - own_hat * row_total / width
+        jnp.sum(normal_partial * norm_gain * (plain * rstd), axis=-1, keepdims=True), "head"
+    )
+    normal_grad = lax.psum_scatter(
+        normal_partial.astype(jnp.bfloat16), "head", scatter_dimension=2, tiled=True
+    ).astype(jnp.float32)
+    back = rstd * (normal_grad * gain_share - own_hat * row_total / width)
+    token_grad = cotangent.astype(jnp.float32) + regroup(back.astype(jnp.bfloat16)).astype(
+        jnp.float32
     )
     norm_gain_part = jnp.sum(normal_grad * own_hat, axis=(0, 1))
     gate_partial = row_product(flat_in, gate_low_flat)
@@ -298,10 +327,10 @@
     )
     state_partial = row_product(own_rows, state_low_flat)
     gate_matrix_grad, value_matrix_grad, step_matrix_grad, output_matrix_grad = (
-        lax.psum_scatter(gate_partial, "seq", scatter_dimension=0, tiled=True),
-        lax.psum_scatter(value_partial, "seq", scatter_dimension=0, tiled=True),
+        summed_low(gate_partial, 0),
+        summed_low(value_partial, 0),
         lax.psum_scatter(step_partial, "seq", scatter_dimension=0, tiled=True),
-        lax.psum_scatter(output_partial, "seq", scatter_dimension=1, tiled=True),
+        summed_low(output_partial, 1),
     )
     summed = lax.psum(
         (

time: 1530 us -> 833 us (0.54)
  waiting for transfers between devices: 1070 us -> 383 us
  local copies, waits for them, and re-layouts: 50.3 us -> 78.1 us
  blocking collectives: 95.6 us -> 69.9 us
  matrix products: 171 us -> 147 us
  starting transfers between devices: 11.1 us -> 29.1 us
    all_gather x4 -> x2, waiting for transfers between devices: 431 us -> 16.9 us  [the longest x1 16.9 us: local(): lax.all_gather(regroup(tokens), 'head', axis=2, tiled=True)]
    reduce_scatter x5, waiting for transfers between devices: 498 us -> 245 us  [the longest x3 245 us: summed_low(): lax.psum_scatter(low, 'seq', scatter_dimension=dim, tiled=True)]
    reduce_scatter x1, waiting for transfers between devices: 64.4 us -> 21.5 us  [local(): lax.psum_scatter(step_partial, 'seq', scatter_dimension=0, tiled=True)]
    reshape x2 -> x6, local copies, waits for them, and re-layouts: 5.65 us -> 38.7 us  [the longest x3 23.5 us: local(): x_grad.reshape(1, row_count, inner_local)]
    all_gather x1 -> x0, blocking collectives: 27.1 us -> none  [prefix(): gathered = jax.tree.map(lambda a: lax.all_gather(a, axis), part)]
    add x7 -> x2, other arithmetic: 26.7 us -> 5.43 us  [depthwise(): summed + kernel[tap_index] * padded[:, tap_index:tap_index + length]]
    all_to_all x0 -> x1, blocking collectives: none -> 20.2 us  [regroup(): lax.all_to_all(block, 'seq', 0, 0, axis_index_groups=groups, tiled=True)]
    all_to_all x0 -> x3, waiting for transfers between devices: none -> 17.6 us  [regroup(): lax.all_to_all(block, 'seq', 0, 0, axis_index_groups=groups, tiled=True)]
  transfers between devices with their start and end apart: 16 -> 19, of which waited for: 11 -> 10; matrix products, arithmetic and copies ran while one was open for 14% -> 30% of each run, Pallas kernels for 0% -> 0%
where the time goes in v1:
time: 833 us; the launch traced here: 823 us
  waiting for transfers between devices  383 us (46%)
  matrix products  147 us (18%)
  other arithmetic  99.9 us (12%)
  local copies, waits for them, and re-layouts  78.1 us (9%)
  blocking collectives  69.9 us (8%)
  starting transfers between devices  29.1 us (3%)
  between operations  16.1 us (2%)
    reduce_scatter x3, waiting for transfers between devices, summed_low(): lax.psum_scatter(low, 'seq', scatter_dimension=dim, tiled=True)  245 us
    psum x1, waiting for transfers between devices, local(): lax.psum((state_partial, norm_gain_part, value_kernel_part, value_bias_pa...  75.3 us
    dot_general x5, matrix products, back_product(): jnp.einsum('rc,dc->rd', grad_rows, matrix, preferred_element_type=jnp.flo...  47.5 us
    psum x1, blocking collectives, local(): lax.psum((state_partial, norm_gain_part, value_kernel_part, value_bias_pa...  36.9 us
    dot_general x4, matrix products, row_product(): jnp.einsum('rd,rc->dc', rows_in, grad_rows, preferred_element_type=jnp.fl...  24.2 us
    reshape x3, local copies, waits for them, and re-layouts, local(): x_grad.reshape(1, row_count, inner_local)  23.5 us
    reduce_scatter x1, waiting for transfers between devices, local(): lax.psum_scatter(step_partial, 'seq', scatter_dimension=0, tiled=True)  21.5 us
    all_to_all x1, blocking collectives, regroup(): lax.all_to_all(block, 'seq', 0, 0, axis_index_groups=groups, tiled=True)  20.2 us
  transfers between devices with their start and end apart: 19, of which 10 were waited for; matrix products, arithmetic and copies ran while one was open for 30% of the time, Pallas kernels for 0%

profile of v1, /device:TPU:0, one launch (start us, length us, event | category | flops | bytes accessed | tf_op | source)
XLA Modules:
  0.0 822.9 jit_solution(8294376757675896777)
XLA Ops:
  7.3 20.2 %all_to_all.20 = bf16[4,256,512]{2,1,0:T(8,128)(2,1)} all-to-all(bf16[4,256,512]{2,1,0:T(8,128)(2,1)} %param.16), channel_id=1, replica_groups={{0,4,8,12},{16,20,24,28},{1,5,9,13},{17,21,25,29},{2,6,10,14},{18,22,26..., dimensions={0} | all-to-all | bytes 2097152 | tf_op jit(solution)/shard_map/all_to_all | solution.py:20
  31.8 12.2 %all-to-all-done.1 = bf16[4,256,512]{2,1,0:T(8,128)(2,1)S(1)} async-done(((bf16[4,256,512]{2,1,0:T(8,128)(2,1)}), bf16[4,256,512]{2,1,0:T(8,128)(2,1)S(1)}, u32[]{:S(2)}, u32[]{:S(2)}) %all-to-all-start.1) | async-done | bytes 1048608 | tf_op jit(solution)/shard_map/all_to_all | solution.py:20
  45.0 16.9 %all-gather.3.cloned.1.call-done = bf16[4,256,2048]{2,1,0:T(8,128)(2,1)} async-done(((bf16[4,256,512]{2,1,0:T(8,128)(2,1)}), bf16[4,256,2048]{2,1,0:T(8,128)(2,1)}) %all-gather.3.cloned.1.call-update) | async-done | bytes 4194320 | tf_op jit(solution)/shard_map/all_gather | solution.py:107
  76.0 10.3 %fusion.142 = f32[1024,1024]{1,0:T(8,128)} fusion(bf16[1024,2048]{1,0:T(8,128)(2,1)} %bitcast.327, bf16[2048,1024]{1,0:T(8,128)(2,1)} %param.20), kind=kOutput, calls=%fused_computation.248 | convolution fusion | flops 4294967296 | bytes 12582912 | tf_op jit(solution)/shard_map/dot_general | solution.py:117
  118.8 7.7 copy.151
  153.0 14.1 %multiply_reduce_fusion.12 = (f32[4,256]{1,0:T(4,128)S(1)}, f32[4,256]{1,0:T(4,128)S(1)}, f32[4,256,1024]{2,1,0:T(8,128)}, f32[4,256,1024]{2,1,0:T(8,128)}) fusion(f32[1024]{0:T(1024)S(1)} %copy-done.99, f32[4,256,1024]{2,1,0:T(8,128)} %copy.162, f32[4,256,1024]{2,1,0:T(8,128)} %fusion.33, bf16[4,256,2048]{2,1,0:T(8,128)(2,1)} %all-gather.5.cloned.1.call-done, ...), kind=kOutput, calls=%fused_computation.75 | convolution fusion | flops 4305451008 | bytes 25178112 | tf_op jit(solution)/shard_map/rc,dc->rd/dot_general | solution.py:64
  173.7 11.1 %multiply_reduce_fusion.7 = (f32[1024]{0:T(1024)}, bf16[4,256,1024]{2,1,0:T(8,128)(2,1)}, bf16[4,256,1024]{2,1,0:T(8,128)(2,1)}, f32[1024]{0:T(1024)}) fusion(f32[4,256,1024]{2,1,0:T(8,128)} %bitcast.326, f32[4,256,1024]{2,1,0:T(8,128)} %fusion.33, f32[4,256]{1,0:T(4,128)S(1)} %get-tuple-element.67, f32[4,256,1024]{2,1,0:T(8,128)} %get-tuple-element.45, ...), kind=kLoop, calls=%fused_computation.64 | loop fusion | flops 31455232 | bytes 25190400 | tf_op jit(solution)/shard_map/reduce_sum | solution.py:246
  190.9 11.5 %multiply_reduce_fusion.1 = (f32[4,16,256]{2,1,0:T(8,128)}, f32[4,16,256]{2,1,0:T(8,128)}, f32[4,16,256]{2,1,0:T(8,128)}, f32[4,256,256]{2,1,0:T(8,128)}) fusion(f32[4,16,256]{2,1,0:T(8,128)S(1)} %copy.159, f32[4,256,256]{2,1,0:T(8,128)S(1)} %copy-done.50, f32[4,16,256]{2,1,0:T(8,128)S(1)} %copy.157, pred[256,256]{1,0:T(8,128)(4,1)S(1)} %iota_compare_fusion, ...), kind=kOutput, calls=%fused_computation.4 | convolution fusion | flops 582696960 | bytes 6684672 | tf_op jit(solution)/shard_map/sthp,srhp->shtr/dot_general | solution.py:211
  233.1 10.6 %fusion.144 = f32[1024,2048]{1,0:T(8,128)} fusion(bf16[1024,1024]{1,0:T(8,128)(2,1)} %bitcast.351, bf16[2048,1024]{1,0:T(8,128)(2,1)} %param.19), kind=kOutput, calls=%fused_computation.250 | convolution fusion | flops 4294967296 | bytes 14680064 | tf_op jit(solution)/shard_map/rc,dc->rd/dot_general | solution.py:64
  254.6 8.1 copy.199
  270.4 8.9 %multiply_reduce_fusion.10 = (f32[1024]{0:T(1024)S(1)}, f32[1024]{0:T(1024)S(1)}, f32[1024]{0:T(1024)S(1)}, f32[1024]{0:T(1024)S(1)}, f32[1,1024,1024]{2,1,0:T(8,128)S(1)}) fusion(f32[1,1024,1024]{2,1,0:T(8,128)} %bitcast.331, f32[1,3,1024]{2,1,0:T(4,128)S(1)} %collective-permute-done, f32[1,1024,1024]{2,1,0:T(8,128)} %reshape.316, ...), kind=kLoop, calls=%fused_computation.68 | loop fusion | flops 18870272 | bytes 16805888 | tf_op jit(solution)/shard_map/reduce_sum | solution.py:57
  293.8 9.1 %fusion.12 = bf16[1,1024,1024]{2,1,0:T(8,128)(2,1)} fusion(f32[1,3,1024]{2,1,0:T(4,128)S(1)} %collective-permute-done.4, f32[1,1024,1024]{2,1,0:T(8,128)} %copy-done.9, f32[1024]{0:T(1024)S(1)} %bitcast.363, f32[1024]{0:T(1024)S(1)} %bitcast.365, f32[1024]{0:T(1024)S(1)} %bitcast.361, f32[1024]{0:T(1024)S(1)} %bitcast.359), kind=kLoop, calls=%fused_computation.33 | loop fusion | flops 11534336 | bytes 6320128 | tf_op jit(solution)/shard_map/convert_element_type | solution.py:280
  306.2 10.7 %fusion.44 = f32[1024,2048]{1,0:T(8,128)} fusion(bf16[2048,1024]{1,0:T(8,128)(2,1)} %param.20, bf16[1,1024,1024]{2,1,0:T(8,128)(2,1)} %fusion.12), kind=kOutput, calls=%fused_computation.91 | convolution fusion | flops 4294967296 | bytes 14680064 | tf_op jit(solution)/shard_map/rc,dc->rd/dot_general | solution.py:64
  318.8 10.8 %bitcast_convert_fusion.2 = (bf16[4,256,2048]{2,1,0:T(8,128)(2,1)}, f32[1024,2048]{1,0:T(8,128)}) fusion(bf16[1024,16]{0,1:T(8,128)(2,1)S(1)} %bitcast.357, bf16[2048,16]{0,1:T(8,128)(2,1)S(1)} %copy-done.53, f32[1024,2048]{1,0:T(8,128)S(1)} %fusion.92, f32[1024,2048]{1,0:T(8,128)} %fusion.144, f32[1024,2048]{1,0:T(8,128)} %fusion.44), kind=kOutput, calls=%fused_computation.236 | convolution fusion | flops 75497472 | bytes 37847040 | tf_op jit(solution)/shard_map/rc,dc->rd/dot_general | solution.py:64
  330.3 10.2 %bitcast_convert_fusion = bf16[1024,2048]{1,0:T(8,128)(2,1)} fusion(bf16[4,256,2048]{2,1,0:T(8,128)(2,1)} %all-gather.5.cloned.1.call-done, f32[4,256,1024]{2,1,0:T(8,128)} %get-tuple-element.45, f32[4,256]{1,0:T(4,128)S(1)} %copy-done.79, f32[1024]{0:T(1024)S(1)} %copy-done.101), kind=kOutput, calls=%fused_computation.7 | convolution fusion | flops 4300210176 | bytes 12591104 | tf_op jit(solution)/shard_map/ri,rd->id/dot_general | solution.py:200
  340.8 9.9 %bitcast_convert_fusion.1 = bf16[2048,1024]{1,0:T(8,128)(2,1)} fusion(bf16[4,256,2048]{2,1,0:T(8,128)(2,1)} %copy-done.1, bf16[4,256,1024]{2,1,0:T(8,128)(2,1)} %get-tuple-element.48), kind=kOutput, calls=%fused_computation.8 | convolution fusion | flops 4297064448 | bytes 10485760 | tf_op jit(solution)/shard_map/rd,rc->dc/dot_general | solution.py:68
  350.7 9.5 %convolution_convert_fusion = bf16[2048,1024]{1,0:T(8,128)(2,1)} fusion(bf16[1024,2048]{1,0:T(8,128)(2,1)} %bitcast.328, bf16[1,1024,1024]{2,1,0:T(8,128)(2,1)} %fusion.12), kind=kOutput, calls=%fused_computation.80 | convolution fusion | flops 4297064448 | bytes 10485760 | tf_op jit(solution)/shard_map/rd,rc->dc/dot_general | solution.py:68
  377.6 8.6 %all-to-all-start.2 = ((bf16[4,256,512]{2,1,0:T(8,128)(2,1)}), bf16[4,256,512]{2,1,0:T(8,128)(2,1)S(1)}, u32[]{:S(2)}, u32[]{:S(2)}) async-start(bf16[4,256,512]{2,1,0:T(8,128)(2,1)} %reduce-scatter.7.cloned.1.call-done), calls=%async_computation.3 | async-start | bytes 2097152 | tf_op jit(solution)/shard_map/all_to_all | solution.py:20
  424.2 66.1 %reduce-scatter.17.cloned.1.call-done = bf16[1024,256]{1,0:T(8,128)(2,1)} async-done(((bf16[1024,2048]{1,0:T(8,128)(2,1)}), bf16[1024,256]{1,0:T(8,128)(2,1)}) %reduce-scatter.17.cloned.1.call-update) | async-done | bytes 524304 | tf_op jit(solution)/shard_map/reduce_scatter | solution.py:73
  492.4 89.4 %reduce-scatter.11.cloned.1.call-done = bf16[256,1024]{1,0:T(8,128)(2,1)} async-done(((bf16[2048,1024]{1,0:T(8,128)(2,1)}), bf16[256,1024]{1,0:T(8,128)(2,1)}) %reduce-scatter.11.cloned.1.call-update) | async-done | bytes 524304 | tf_op jit(solution)/shard_map/reduce_scatter | solution.py:73
  583.9 89.8 %reduce-scatter.13.cloned.1.call-done = bf16[256,1024]{1,0:T(8,128)(2,1)} async-done(((bf16[2048,1024]{1,0:T(8,128)(2,1)}), bf16[256,1024]{1,0:T(8,128)(2,1)}) %reduce-scatter.13.cloned.1.call-update) | async-done | bytes 524304 | tf_op jit(solution)/shard_map/reduce_scatter | solution.py:73
  675.8 36.9 %all-reduce = (f32[512]{0:T(512)}, f32[4,1024]{1,0:T(4,128)}, f32[1024]{0:T(1024)}, f32[4,256]{1,0:T(4,128)}, f32[256]{0:T(256)}, /*index=5*/f32[16]{0:T(128)}, f32[16]{0:T(128)}, f32[16]{0:T(128)}, f32[1024]{0:T(1024)}) all-reduce(f32[512]{0:T(512)S(1)} %get-tuple-element.49, ...), channel_id=1, replica_groups=mesh['seq'=8,'head'=4] {'seq'}, use_global_device_ids=true, to_apply=%region_23.24 | all-reduce | flops 7984 | bytes 63872 | tf_op jit(solution)/shard_map/psum | solution.py:335
  717.2 21.5 %reduce-scatter.15.cloned.1.call-done = f32[256,16]{0,1:T(8,128)} async-done(((f32[2048,16]{0,1:T(8,128)}), f32[256,16]{0,1:T(8,128)}) %reduce-scatter.15.cloned.1.call-update) | async-done | bytes 16400 | tf_op jit(solution)/shard_map/reduce_scatter | solution.py:332
  738.7 75.3 %all-reduce.6.cloned.1.call-done = f32[512,256]{1,0:T(8,128)} async-done(((f32[512,256]{1,0:T(8,128)}), f32[512,256]{1,0:T(8,128)}) %all-reduce.6.cloned.1.call-update) | async-done | bytes 524304 | tf_op jit(solution)/shard_map/psum | solution.py:335
  (383 shorter events, 227.6 us)
Async XLA Ops:
  7.2 54.7 %all-gather.3.cloned.1.call-start = ((), (), s32[]{:S(2)}) async-start(), calls=%async_computation.10 | async-start | bytes 5242880 | tf_op jit(solution)/shard_map/all_gather | solution.py:107
  27.5 16.5 %all-to-all-start.1 = ((bf16[4,256,512]{2,1,0:T(8,128)(2,1)}), bf16[4,256,512]{2,1,0:T(8,128)(2,1)S(1)}, u32[]{:S(2)}, u32[]{:S(2)}) async-start(bf16[4,256,512]{2,1,0:T(8,128)(2,1)} %param.17), calls=%async_computation.1 | async-start | bytes 2097152 | tf_op jit(solution)/shard_map/all_to_all | solution.py:20
  31.0 122.0 %all-gather.5.cloned.1.call-start = ((), (), s32[]{:S(2)}) async-start(), calls=%async_computation.11 | async-start | bytes 5242880 | tf_op jit(solution)/shard_map/all_gather | solution.py:108
  31.7 159.2 %copy-start.60 = (pred[256,256]{1,0:T(8,128)(4,1)}, pred[256,256]{1,0:T(8,128)(4,1)S(1)}, u32[]{:S(2)}) copy-start(pred[256,256]{1,0:T(8,128)(4,1)S(1)} %iota_compare_fusion) | copy-start | bytes 196612
  45.0 257.8 %all-reduce.4.cloned.1.call-start = ((), (), s32[]{:S(2)}) async-start(), calls=%async_computation.13 | async-start | bytes 2097152 | tf_op jit(solution)/shard_map/psum | solution.py:268
  88.1 16.5 %collective-permute-start.1 = (f32[1,3,256]{2,1,0:T(4,128)}, f32[1,3,256]{2,1,0:T(4,128)S(1)}, u32[]{:S(2)}, u32[]{:S(2)}) collective-permute-start(f32[1,3,256]{2,1,0:T(4,128)} %slice.205), channel_id=1, source_target_pairs={{0,16},{4,20},{8,24},{12,28},{1,17},{5,21},{9,25},{13,29},{2,18},{... | collective-permute-start | bytes 9224 | tf_op jit(solution)/shard_map/ppermute | solution.py:13
  100.5 6.8 collective-permute-start
  103.4 87.5 %copy-start.56 = (f32[4,16,256]{2,1,0:T(8,128)}, f32[4,16,256]{2,1,0:T(8,128)S(1)}, u32[]{:S(2)}) copy-start(f32[4,16,256]{2,1,0:T(8,128)S(1)} %copy.157) | copy-start | bytes 196612
  130.9 7.3 collective-permute-start.2
  216.3 10.9 %collective-permute-start.3 = (bf16[16,64,128]{2,1,0:T(8,128)(2,1)}, bf16[16,64,128]{2,1,0:T(8,128)(2,1)S(1)}, u32[]{:S(2)}, u32[]{:S(2)}) collective-permute-start(bf16[16,64,128]{2,1,0:T(8,128)(2,1)} %fusion.79), channel_id=1, source_target_pairs={{16,0},{20,4},{24,8},{28,12},{17,1},{21,5},{25,9},{29,13},{18,2},{... | collective-permute-start | bytes 786440 | tf_op jit(solution)/shard_map/ppermute | solution.py:13
  233.1 144.5 %reduce-scatter.7.cloned.1.call-start = ((), (), s32[]{:S(2)}) async-start(), calls=%async_computation.12 | async-start | bytes 5242880 | tf_op jit(solution)/shard_map/reduce_scatter | solution.py:194
  243.8 159.5 %reduce-scatter.9.cloned.1.call-start = ((), (), s32[]{:S(2)}) async-start(), calls=%async_computation.14 | async-start | bytes 5242880 | tf_op jit(solution)/shard_map/reduce_scatter | solution.py:314
  281.3 12.4 %collective-permute-start.4 = (f32[1,3,1024]{2,1,0:T(4,128)S(1)}, f32[1,3,1024]{2,1,0:T(4,128)S(1)}, u32[]{:S(2)}, u32[]{:S(2)}) collective-permute-start(f32[1,3,1024]{2,1,0:T(4,128)S(1)} %slice.223), channel_id=1, source_target_pairs={{16,0},{20,4},{24,8},{28,12},{17,1},{21,5},{25,9},{29,13},{18,2},{... | collective-permute-start | bytes 36872 | tf_op jit(solution)/shard_map/ppermute | solution.py:13
  304.5 12.4 %collective-permute-start.5 = (f32[1,3,256]{2,1,0:T(4,128)S(1)}, f32[1,3,256]{2,1,0:T(4,128)S(1)}, u32[]{:S(2)}, u32[]{:S(2)}) collective-permute-start(f32[1,3,256]{2,1,0:T(4,128)S(1)} %slice.228), channel_id=1, source_target_pairs={{16,0},{20,4},{24,8},{28,12},{17,1},{21,5},{25,9},{29,13},{18,2},{... | collective-permute-start | bytes 9224 | tf_op jit(solution)/shard_map/ppermute | solution.py:13
  329.7 160.7 %reduce-scatter.17.cloned.1.call-start = ((), (), s32[]{:S(2)}) async-start(), calls=%async_computation.19 | async-start | bytes 4718592 | tf_op jit(solution)/shard_map/reduce_scatter | solution.py:73
  340.6 241.2 %reduce-scatter.11.cloned.1.call-start = ((), (), s32[]{:S(2)}) async-start(), calls=%async_computation.15 | async-start | bytes 4718592 | tf_op jit(solution)/shard_map/reduce_scatter | solution.py:73
  350.7 323.0 %reduce-scatter.13.cloned.1.call-start = ((), (), s32[]{:S(2)}) async-start(), calls=%async_computation.16 | async-start | bytes 4718592 | tf_op jit(solution)/shard_map/reduce_scatter | solution.py:73
  377.6 34.8 %all-to-all-start.2 = ((bf16[4,256,512]{2,1,0:T(8,128)(2,1)}), bf16[4,256,512]{2,1,0:T(8,128)(2,1)S(1)}, u32[]{:S(2)}, u32[]{:S(2)}) async-start(bf16[4,256,512]{2,1,0:T(8,128)(2,1)} %reduce-scatter.7.cloned.1.call-done), calls=%async_computation.3 | async-start | bytes 2097152 | tf_op jit(solution)/shard_map/all_to_all | solution.py:20
  413.4 300.6 %all-to-all-start.3 = ((bf16[4,256,512]{2,1,0:T(8,128)(2,1)}), bf16[4,256,512]{2,1,0:T(8,128)(2,1)}, u32[]{:S(2)}, u32[]{:S(2)}) async-start(bf16[4,256,512]{2,1,0:T(8,128)(2,1)} %get-tuple-element.50), calls=%async_computation.5 | async-start | bytes 2097152 | tf_op jit(solution)/shard_map/all_to_all | solution.py:20
  417.8 320.9 %reduce-scatter.15.cloned.1.call-start = ((), (), s32[]{:S(2)}) async-start(), calls=%async_computation.18 | async-start | bytes 147456 | tf_op jit(solution)/shard_map/reduce_scatter | solution.py:332
  421.5 392.5 %all-reduce.6.cloned.1.call-start = ((), (), s32[]{:S(2)}) async-start(), calls=%async_computation.17 | async-start | bytes 1048576 | tf_op jit(solution)/shard_map/psum | solution.py:335
  422.2 253.6 %copy-start.80 = (f32[1024]{0:T(1024)S(1)}, f32[1024]{0:T(1024)}, u32[]{:S(2)}) copy-start(f32[1024]{0:T(1024)} %get-tuple-element.51) | copy-start | bytes 12292
  422.2 290.5 %copy-start.38 = (bf16[4,256,512]{2,1,0:T(8,128)(2,1)S(1)}, bf16[4,256,512]{2,1,0:T(8,128)(2,1)}, u32[]{:S(2)}) copy-start(bf16[4,256,512]{2,1,0:T(8,128)(2,1)} %param.16) | copy-start | bytes 3145732
  422.2 290.5 %copy-start.40 = (bf16[4,256,512]{2,1,0:T(8,128)(2,1)S(1)}, bf16[4,256,512]{2,1,0:T(8,128)(2,1)}, u32[]{:S(2)}) copy-start(bf16[4,256,512]{2,1,0:T(8,128)(2,1)} %copy-done.39) | copy-start | bytes 3145732
  (109 other events, 1600.9 us)
Sparse Core Ops, SparseCore 0:
  27.6 34.2 all-gather.2
  64.1 34.4 all-gather.4
  233.2 42.9 all-reduce.3
  278.8 44.8 reduce-scatter.6
  329.8 50.3 reduce-scatter.8
  384.1 106.2 reduce-scatter.16
  493.9 87.7 reduce-scatter.10
  585.8 87.8 reduce-scatter.12
  677.6 61.0 reduce-scatter.14
  742.5 71.4 all-reduce.5

commit v2 on v1

v2 whole, which is shorter than its diff:
```python
import jax
import jax.numpy as jnp
from jax import lax
from jax.experimental import pallas as pl
from jax.experimental.pallas import tpu as pltpu
from jax.sharding import PartitionSpec as P

HIGH = lax.Precision.HIGHEST
EPSILON = 1e-05
F32 = jnp.float32
BF16 = jnp.bfloat16
LANES = 128
EDGE = 8
VMEM_BYTES = 56 * 1024 * 1024

NN = (((1,), (0,)), ((), ()))
NT = (((1,), (1,)), ((), ()))
TN = (((0,), (0,)), ((), ()))


def dot(a, b, dims=NN, precision=None):
    return lax.dot_general(a, b, dims, precision=precision, preferred_element_type=F32)


def dot_split(a, b, dims=NN):
    high = a.astype(BF16)
    rest = (a - high.astype(F32)).astype(BF16)
    return dot(high, b, dims) + dot(rest, b, dims)


def sigmoid(v):
    return 1.0 / (1.0 + jnp.exp(-v))


def silu(v):
    return v * sigmoid(v)


def slope(v):
    sigma = sigmoid(v)
    return sigma * (1.0 + v * (1.0 - sigma))


def softplus(v):
    return jnp.maximum(v, 0.0) + jnp.log1p(jnp.exp(-jnp.abs(v)))


def ones_where(shape, rule):
    rows = lax.broadcasted_iota(jnp.int32, shape, 0)
    cols = lax.broadcasted_iota(jnp.int32, shape, 1)
    return rule(rows, cols)


def head_picker(channels, heads):
    wide = channels // heads
    return ones_where((channels, heads), lambda r, c: r // wide == c).astype(F32).astype(BF16)


def pair_spread(cols, j, rows):
    lane = lax.broadcasted_iota(jnp.int32, (rows, LANES), 1)
    first = jnp.broadcast_to(cols[:, 2 * j : 2 * j + 1], (rows, LANES))
    second = jnp.broadcast_to(cols[:, 2 * j + 1 : 2 * j + 2], (rows, LANES))
    return jnp.where(lane < LANES // 2, first, second)


def spread(cols, rows, heads):
    return jnp.concatenate([pair_spread(cols, j, rows) for j in range(heads // 2)], axis=1)


def call(kernel, name, grid, in_specs, out_specs, out_shape, scratch, flops, args, transcendentals=0):
    moved = sum(a.size * a.dtype.itemsize for a in args) + sum(
        o.size * o.dtype.itemsize for o in out_shape
    )
    return pl.pallas_call(
        kernel,
        grid=grid,
        in_specs=in_specs,
        out_specs=out_specs,
        out_shape=out_shape,
        scratch_shapes=scratch,
        compiler_params=pltpu.CompilerParams(
            dimension_semantics=("arbitrary",) * len(grid), vmem_limit_bytes=VMEM_BYTES
        ),
        cost_estimate=pl.CostEstimate(
            flops=int(flops), bytes_accessed=int(moved), transcendentals=int(transcendentals)
        ),
        name=name,
    )(*args)


def shape(dims, dtype):
    return jax.ShapeDtypeStruct(dims, dtype)


def prepare(value_pre, value_edge, state_pre, state_edge, step_pre, value_kernel, value_bias,
            state_kernel, state_bias, step_bias, log_rate, length):
    rows, channels = value_pre.shape
    heads = step_pre.shape[1]
    both = state_pre.shape[1]
    states = both // 2
    wide = channels // heads
    count = rows // length
    taps = value_kernel.shape[0]
    unit = length // EDGE

    def kernel(xr, xr_before, xr_edge, bc, bc_before, bc_edge, dtr, vk, vb, sk, sb, tb, lr,
               xs_o, xdt_o, xw_o, bcs_o, dt_o, cum_o, cumt_o, hin_o, pre_o, dec_o, end_o,
               padded, padded_bc, state, ahead):
        i = pl.program_id(0)

        @pl.when(i == 0)
        def _():
            padded[0:EDGE] = xr_edge[...]
            padded_bc[0:EDGE] = bc_edge[...]
            state[...] = jnp.zeros_like(state)
            ahead[...] = jnp.ones_like(ahead)

        @pl.when(i > 0)
        def _():
            padded[0:EDGE] = xr_before[...]
            padded_bc[0:EDGE] = bc_before[...]

        padded[EDGE:] = xr[...]
        padded_bc[EDGE:] = bc[...]
        start = EDGE - taps + 1
        summed = sb[...] + sk[0:1] * padded_bc[pl.ds(start, length)]
        for k in range(1, taps):
            summed = summed + sk[k : k + 1] * padded_bc[pl.ds(start + k, length)]
        basis = silu(summed).astype(BF16)
        bcs_o[...] = basis
        dt = softplus(dtr[...] + tb[...])
        da = dt * -jnp.exp(lr[...])
        lower = ones_where((length, length), lambda r, c: r >= c).astype(F32)
        upper = ones_where((length, length), lambda r, c: r <= c).astype(F32)
        cum = dot(lower, da, precision=HIGH)
        cumt = dot(da, upper, TN, precision=HIGH)
        dt_o[...] = dt
        cum_o[...] = cum
        cumt_o[...] = cumt
        factor = jnp.exp(cum[length - 1 : length] - cum) * dt
        decay = jnp.exp(jnp.broadcast_to(cumt[:, length - 1 : length], (heads, LANES)))
        dec_o[0] = decay
        pre_o[0] = ahead[...]
        ahead[...] = ahead[...] * decay
        hin_o[0] = state[...]
        for j in range(channels // LANES):
            at = slice(j * LANES, (j + 1) * LANES)
            total = vb[:, at] + vk[0:1, at] * padded[pl.ds(start, length), at]
            for k in range(1, taps):
                total = total + vk[k : k + 1, at] * padded[pl.ds(start + k, length), at]
            xs = silu(total).astype(BF16)
            xs_o[:, at] = xs
            plain = xs.astype(F32)
            xdt_o[:, at] = (plain * pair_spread(dt, j, length)).astype(BF16)
            xw_o[:, at] = (plain * pair_spread(factor, j, length)).astype(BF16)
        local = dot(xw_o[...], basis[:, :states], TN)
        for h in range(heads):
            at = slice(h * wide, (h + 1) * wide)
            state[at] = decay[h : h + 1] * state[at] + local[at]
        end_o[...] = state[...].astype(BF16)

    whole = lambda *dims: pl.BlockSpec(dims, lambda i: (0,) * len(dims))
    tokens = lambda n: pl.BlockSpec((length, n), lambda i: (i, 0))
    before = lambda n: pl.BlockSpec((EDGE, n), lambda i: (jnp.maximum(i * unit - 1, 0), 0))
    per = lambda *dims: pl.BlockSpec((1,) + dims, lambda i: (i, 0, 0))
    return call(
        kernel, "conv_and_local_states", (count,),
        [tokens(channels), before(channels), whole(EDGE, channels), tokens(both), before(both),
         whole(EDGE, both), tokens(heads), whole(taps, channels), whole(1, channels),
         whole(taps, both), whole(1, both), whole(1, heads), whole(1, heads)],
        [tokens(channels), tokens(channels), tokens(channels), tokens(both), tokens(heads),
         tokens(heads), pl.BlockSpec((heads, length), lambda i: (0, i)), per(channels, states),
         per(heads, LANES), per(heads, LANES), whole(channels, states)],
        [shape((rows, channels), BF16), shape((rows, channels), BF16), shape((rows, channels), BF16),
         shape((rows, both), BF16), shape((rows, heads), F32), shape((rows, heads), F32),
         shape((heads, rows), F32), shape((count, channels, states), F32),
         shape((count, heads, LANES), F32), shape((count, heads, LANES), F32),
         shape((channels, states), BF16)],
        [pltpu.VMEM((length + EDGE, channels), F32), pltpu.VMEM((length + EDGE, both), F32),
         pltpu.VMEM((channels, states), F32), pltpu.VMEM((heads, LANES), F32)],
        2 * rows * channels * states,
        (value_pre, value_pre, value_edge, state_pre, state_pre, state_edge, step_pre, value_kernel,
         value_bias, state_kernel, state_bias, step_bias, log_rate),
        4 * rows * channels,
    )


def decays(cum, cumt, h, half):
    top = jnp.exp(jnp.minimum(cum[:half, h : h + 1] - cumt[h : h + 1, :half], 0.0))
    low = jnp.exp(jnp.minimum(cum[half:, h : h + 1] - cumt[h : h + 1, :], 0.0))
    return top, low


def lower_scores(basis, states, length):
    scores = dot(basis[:, states:], basis[:, :states], NT)
    return jnp.where(ones_where((length, length), lambda r, c: r >= c), scores, 0.0)


def intra(bcs, xdt, cum, cumt, length):
    rows, channels = xdt.shape
    heads = cum.shape[1]
    both = bcs.shape[1]
    states = both // 2
    half = length // 2

    def kernel(bcs_r, xdt_r, cum_r, cumt_r, y_o):
        scores = lower_scores(bcs_r[...], states, length)
        cum_v, cumt_v = cum_r[...], cumt_r[...]
        lane = lax.broadcasted_iota(jnp.int32, (length, LANES), 1)
        for j in range(heads // 2):
            at = slice(j * LANES, (j + 1) * LANES)
            pair = xdt_r[:, at]
            y_top = jnp.zeros((half, LANES), F32)
            y_low = jnp.zeros((half, LANES), F32)
            for s in range(2):
                own = jnp.where((lane < LANES // 2) == (s == 0), pair, jnp.zeros_like(pair))
                top, low = decays(cum_v, cumt_v, 2 * j + s, half)
                y_top += dot((scores[:half, :half] * top).astype(BF16), own[:half])
                y_low += dot((scores[half:] * low).astype(BF16), own)
            y_o[:half, at] = y_top
            y_o[half:, at] = y_low

    tokens = lambda n: pl.BlockSpec((length, n), lambda i: (i, 0))
    return call(
        kernel, "within_blocks", (rows // length,),
        [tokens(both), tokens(channels), tokens(heads), pl.BlockSpec((heads, length), lambda i: (0, i))],
        [tokens(channels)], [shape((rows, channels), F32)], [],
        2 * rows * length * channels * 4, (bcs, xdt, cum, cumt), rows * length * heads,
    )[0]


def finish(y_intra, xs, bcs, gate_pre, normed_grad, cum, hin0, pre, carry, skip_row, gate_gain, length):
    rows, channels = xs.shape
    heads = cum.shape[1]
    both = bcs.shape[1]
    states = both // 2
    wide = channels // heads
    count = rows // length

    def kernel(yi, xs_r, bcs_r, z, dn, cum_r, hin_r, pre_r, carry_r, skip, gain, y_o, low_o, sums_o):
        for h in range(heads):
            at = slice(h * wide, (h + 1) * wide)
            low_o[0, at] = (hin_r[0, at] + pre_r[0, h : h + 1] * carry_r[at].astype(F32)).astype(BF16)
        growth = jnp.exp(cum_r[...])
        squares = jnp.zeros((length, LANES), F32)
        crosses = jnp.zeros((length, LANES), F32)
        out_basis = bcs_r[:, states:]
        for j in range(channels // LANES):
            at = slice(j * LANES, (j + 1) * LANES)
            v = dot(out_basis, low_o[0, at], NT)
            y = yi[:, at] + pair_spread(growth, j, length) * v + skip[:, at] * xs_r[:, at].astype(F32)
            y_o[:, at] = y
            gated = y * silu(z[:, at])
            squares += gated * gated
            crosses += dn[:, at] * gain[:, at] * gated
        sums_o[...] = jnp.concatenate(
            [jnp.sum(squares, axis=1, keepdims=True), jnp.sum(crosses, axis=1, keepdims=True)], axis=1
        )

    whole = lambda *dims: pl.BlockSpec(dims, lambda i: (0,) * len(dims))
    tokens = lambda n: pl.BlockSpec((length, n), lambda i: (i, 0))
    per = lambda *dims: pl.BlockSpec((1,) + dims, lambda i: (i, 0, 0))
    return call(
        kernel, "across_blocks", (count,),
        [tokens(channels), tokens(channels), tokens(both), tokens(channels), tokens(channels),
         tokens(heads), per(channels, states), per(heads, LANES), whole(channels, states),
         whole(1, channels), whole(1, channels)],
        [tokens(channels), per(channels, states), tokens(2)],
        [shape((rows, channels), F32), shape((count, channels, states), BF16), shape((rows, 2), F32)],
        [], 2 * rows * channels * states,
        (y_intra, xs, bcs, gate_pre, normed_grad, cum, hin0, pre, carry, skip_row, gate_gain),
        2 * rows * channels,
    )


def turn(y, gate_pre, normed_grad, xs, bcs, cum, sums, gate_gain, output_matrix, dec, length, inner):
    rows, channels = xs.shape
    heads = cum.shape[1]
    both = bcs.shape[1]
    states = both // 2
    wide = channels // heads
    count = rows // length
    width = output_matrix.shape[1]

    def kernel(y_r, z_r, dn_r, xs_r, bcs_r, cum_r, sums_r, gain, wo, dec_r,
               normed_o, part_o, dy_o, dz_o, dv_o, ab_o, ds_o, post_o, start_o, ggain_o,
               state, behind, prod_a, prod_b):
        i = pl.program_id(0)

        @pl.when(i == 0)
        def _():
            state[...] = jnp.zeros_like(state)
            behind[...] = jnp.ones_like(behind)
            ggain_o[...] = jnp.zeros_like(ggain_o)

        grstd = lax.rsqrt(sums_r[:, 0:1] / inner + EPSILON)
        cross = (grstd * grstd * grstd) * (sums_r[:, 1:2] / inner)
        growth = jnp.exp(cum_r[...])
        for j in range(channels // LANES):
            at = slice(j * LANES, (j + 1) * LANES)
            y, z, dn = y_r[:, at], z_r[:, at], dn_r[:, at]
            sigma = sigmoid(z)
            act = z * sigma
            gated = y * act
            scaled = gated * grstd
            normed_o[:, at] = (scaled * gain[:, at]).astype(BF16)
            ggain_o[:, at] += jnp.sum(dn * scaled, axis=0, keepdims=True)
            dgated = grstd * (dn * gain[:, at]) - gated * cross
            dy = (dgated * act).astype(BF16)
            dy_o[:, at] = dy
            dz_o[:, at] = (dgated * y * (sigma * (1.0 + z * (1.0 - sigma)))).astype(BF16)
            plain = dy.astype(F32)
            dv_o[:, at] = (plain * pair_spread(growth, j, length)).astype(BF16)
            prod_a[:, at] = plain * y
            prod_b[:, at] = plain * xs_r[:, at].astype(F32)
        picker = head_picker(channels, heads)
        ab_o[:, :heads] = dot_split(prod_a[...], picker)
        ab_o[:, heads:] = dot_split(prod_b[...], picker)
        part_o[...] = dot(normed_o[...], wo[...]).astype(BF16)
        dhin = dot(dv_o[...], bcs_r[:, states:], TN)
        ds_o[0] = state[...]
        post_o[0] = behind[...]
        behind[...] = behind[...] * dec_r[0]
        for h in range(heads):
            at = slice(h * wide, (h + 1) * wide)
            state[at] = dec_r[0, h : h + 1] * state[at] + dhin[at]
        start_o[...] = state[...].astype(BF16)

    last = count - 1
    whole = lambda *dims: pl.BlockSpec(dims, lambda i: (0,) * len(dims))
    tokens = lambda n: pl.BlockSpec((length, n), lambda i: (last - i, 0))
    per = lambda *dims: pl.BlockSpec((1,) + dims, lambda i: (last - i, 0, 0))
    return call(
        kernel, "gate_and_turn", (count,),
        [tokens(channels), tokens(channels), tokens(channels), tokens(channels), tokens(both),
         tokens(heads), tokens(2), whole(1, channels), whole(channels, width), per(heads, LANES)],
        [tokens(channels), tokens(width), tokens(channels), tokens(channels), tokens(channels),
         tokens(2 * heads), per(channels, states), per(heads, LANES), whole(channels, states),
         whole(1, channels)],
        [shape((rows, channels), BF16), shape((rows, width), BF16), shape((rows, channels), BF16),
         shape((rows, channels), BF16), shape((rows, channels), BF16), shape((rows, 2 * heads), F32),
         shape((count, channels, states), F32), shape((count, heads, LANES), F32),
         shape((channels, states), BF16), shape((1, channels), F32)],
        [pltpu.VMEM((channels, states), F32), pltpu.VMEM((heads, LANES), F32),
         pltpu.VMEM((length, channels), F32), pltpu.VMEM((length, channels), F32)],
        2 * rows * channels * (width + states),
        (y, gate_pre, normed_grad, xs, bcs, cum, sums, gate_gain, output_matrix, dec),
        rows * channels,
    )


def intra_back(bcs, xdt, dy, cum, cumt, length):
    rows, channels = xdt.shape
    heads = cum.shape[1]
    both = bcs.shape[1]
    states = both // 2
    half = length // 2

    def kernel(bcs_r, xdt_r, dy_r, cum_r, cumt_r, g_o, dbc_o, grad):
        scores = lower_scores(bcs_r[...], states, length)
        cum_v, cumt_v = cum_r[...], cumt_r[...]
        lane = lax.broadcasted_iota(jnp.int32, (length, LANES), 1)
        grad[...] = jnp.zeros_like(grad)
        for j in range(heads // 2):
            at = slice(j * LANES, (j + 1) * LANES)
            pair, dpair = xdt_r[:, at], dy_r[:, at]
            g_top = jnp.zeros((half, LANES), F32)
            g_low = jnp.zeros((half, LANES), F32)
            for s in range(2):
                own = jnp.where((lane < LANES // 2) == (s == 0), dpair, jnp.zeros_like(dpair))
                top, low = decays(cum_v, cumt_v, 2 * j + s, half)
                grad[:half, :half] += dot(own[:half], pair[:half], NT) * top
                grad[half:] += dot(own[half:], pair, NT) * low
                w_top = (scores[:half, :half] * top).astype(BF16)
                w_low = (scores[half:] * low).astype(BF16)
                g_top += dot(w_top, own[:half], TN) + dot(w_low[:, :half], own[half:], TN)
                g_low += dot(w_low[:, half:], own[half:], TN)
            g_o[:half, at] = g_top
            g_o[half:, at] = g_low
        masked = jnp.where(ones_where((length, length), lambda r, c: r >= c), grad[...], 0.0)
        high = masked.astype(BF16)
        rest = (masked - high.astype(F32)).astype(BF16)
        in_b, out_b = bcs_r[:, :states], bcs_r[:, states:]
        dbc_o[:, :states] = dot(high, out_b, TN) + dot(rest, out_b, TN)
        dbc_o[:, states:] = dot(high, in_b) + dot(rest, in_b)

    tokens = lambda n: pl.BlockSpec((length, n), lambda i: (i, 0))
    return call(
        kernel, "within_blocks_back", (rows // length,),
        [tokens(both), tokens(channels), tokens(channels), tokens(heads),
         pl.BlockSpec((heads, length), lambda i: (0, i))],
        [tokens(channels), tokens(both)],
        [shape((rows, channels), F32), shape((rows, both), F32)],
        [pltpu.VMEM((length, length), F32)],
        2 * rows * length * channels * 8, (bcs, xdt, dy, cum, cumt), rows * length * heads,
    )


def finish_back(value_pre, value_edge, value_kernel, value_bias, xs, xdt, xw, g, dy, dv, bcs, step_pre, dt,
                cum, ab, hin0, pre, carry, hin_low, ds0, post, back, dec, dbc_intra, skip_row, skip_gain,
                step_bias, log_rate, length):
    rows, channels = xs.shape
    heads = cum.shape[1]
    both = bcs.shape[1]
    states = both // 2
    wide = channels // heads
    count = rows // length
    taps = value_kernel.shape[0]
    unit = length // EDGE

    def kernel(xr, xr_before, xr_edge, vk, vb, xs_r, xdt_r, xw_r, g_r, dy_r, dv_r, bcs_r, dtr, dt_r, cum_r,
               ab_r, hin_r, pre_r, carry_r, low_r, ds_r, post_r, back_r, dec_r, dbci, skip, skipg, tb,
               lr, dxr_o, tail_o, head_o, vkg_o, vbg_o, ddtr_o, dbc_o, small_o,
               padded, ext, ds_low, inner_sums):
        i = pl.program_id(0)
        block = count - 1 - i

        @pl.when(i == 0)
        def _():
            vkg_o[...] = jnp.zeros_like(vkg_o)
            vbg_o[...] = jnp.zeros_like(vbg_o)
            small_o[...] = jnp.zeros_like(small_o)
            ext[0:EDGE] = jnp.zeros((EDGE, channels), F32)

        @pl.when(block == 0)
        def _():
            padded[0:EDGE] = xr_edge[...]

        @pl.when(block > 0)
        def _():
            padded[0:EDGE] = xr_before[...]

        padded[EDGE:] = xr[...]
        ext[length:] = ext[0:EDGE]
        for h in range(heads):
            at = slice(h * wide, (h + 1) * wide)
            ds = ds_r[0, at] + post_r[0, h : h + 1] * back_r[at].astype(F32)
            ds_low[at] = ds.astype(BF16)
            hin = hin_r[0, at] + pre_r[0, h : h + 1] * carry_r[at].astype(F32)
            inner_sums[h : h + 1] = jnp.sum(ds * hin, axis=0, keepdims=True) * dec_r[0, h : h + 1]
        in_b = bcs_r[:, :states]
        dt_v, cum_v = dt_r[...], cum_r[...]
        fade = jnp.exp(cum_v[length - 1 : length] - cum_v)
        factor = fade * dt_v
        start = EDGE - taps + 1
        picker = head_picker(channels, heads)
        c_sum = jnp.zeros((length, heads), F32)
        d_sum = jnp.zeros((length, heads), F32)
        w_sum = jnp.zeros((length, heads), F32)
        for j in range(channels // LANES):
            at = slice(j * LANES, (j + 1) * LANES)
            xs_v = xs_r[:, at].astype(F32)
            dxw = dot(in_b, ds_low[at], NT)
            g_v = g_r[:, at]
            c_sum += dot_split(xs_v * g_v, picker[at])
            d_sum += dot_split(xs_v * dxw, picker[at])
            w_sum += dot_split(xdt_r[:, at].astype(F32) * g_v, picker[at])
            dxs = (
                pair_spread(dt_v, j, length) * g_v
                + pair_spread(factor, j, length) * dxw
                + skip[:, at] * dy_r[:, at].astype(F32)
            )
            total = vb[:, at] + vk[0:1, at] * padded[pl.ds(start, length), at]
            for k in range(1, taps):
                total = total + vk[k : k + 1, at] * padded[pl.ds(start + k, length), at]
            dpre = dxs * slope(total)
            ext[0:length, at] = dpre
            vbg_o[:, at] += jnp.sum(dpre, axis=0, keepdims=True)
            for k in range(taps):
                vkg_o[k : k + 1, at] += jnp.sum(
                    dpre * padded[pl.ds(start + k, length), at], axis=0, keepdims=True
                )
            dxr = vk[0:1, at] * ext[pl.ds(taps - 1, length), at]
            for k in range(1, taps):
                dxr = dxr + vk[k : k + 1, at] * ext[pl.ds(taps - 1 - k, length), at]
            dxr_o[:, at] = dxr.astype(BF16)

            @pl.when(i == 0)
            def _():
                tail_o[:, at] = dxr[length - EDGE :]

        head_o[...] = ext[0:EDGE]
        dbc_o[:, :states] = dbci[:, :states] + dot(xw_r[...], ds_low[...])
        dbc_o[:, states:] = dbci[:, states:] + dot(dv_r[...], low_r[0])
        rate = -jnp.exp(lr[...])
        a_sum, b_sum = ab_r[:, :heads], ab_r[:, heads:]
        e_sum = d_sum * factor
        ones = jnp.ones((1, LANES), F32)
        dtotal = jnp.sum(e_sum, axis=0, keepdims=True) + dot(ones, inner_sums[...], NT, precision=HIGH)
        row = lax.broadcasted_iota(jnp.int32, (length, heads), 0)
        dcum = a_sum - skipg[...] * b_sum - w_sum - e_sum
        dcum = dcum + jnp.where(row == length - 1, dtotal, 0.0)
        upper = ones_where((length, length), lambda r, c: r <= c).astype(F32)
        dda = dot(upper, dcum, precision=HIGH)
        ddt = c_sum + d_sum * fade + dda * rate
        dpre_dt = ddt * sigmoid(dtr[...] + tb[...])
        ddtr_o[...] = dpre_dt.astype(BF16)
        small_o[0:1] += jnp.sum(dpre_dt, axis=0, keepdims=True)
        small_o[1:2] += jnp.sum(dda * dt_v, axis=0, keepdims=True) * rate
        small_o[2:3] += jnp.sum(b_sum, axis=0, keepdims=True)

    last = count - 1
    whole = lambda *dims: pl.BlockSpec(dims, lambda i: (0,) * len(dims))
    tokens = lambda n: pl.BlockSpec((length, n), lambda i: (last - i, 0))
    before = lambda n: pl.BlockSpec((EDGE, n), lambda i: (jnp.maximum((last - i) * unit - 1, 0), 0))
    per = lambda *dims: pl.BlockSpec((1,) + dims, lambda i: (last - i, 0, 0))
    return call(
        kernel, "across_blocks_back", (count,),
        [tokens(channels), before(channels), whole(EDGE, channels), whole(taps, channels),
         whole(1, channels), tokens(channels), tokens(channels), tokens(channels), tokens(channels),
         tokens(channels), tokens(channels), tokens(both), tokens(heads), tokens(heads), tokens(heads),
         tokens(2 * heads), per(channels, states), per(heads, LANES), whole(channels, states),
         per(channels, states), per(channels, states), per(heads, LANES), whole(channels, states),
         per(heads, LANES), tokens(both), whole(1, channels), whole(1, heads), whole(1, heads),
         whole(1, heads)],
        [tokens(channels), whole(EDGE, channels), whole(EDGE, channels), whole(taps, channels),
         whole(1, channels), tokens(heads), tokens(both), whole(EDGE, heads)],
        [shape((rows, channels), BF16), shape((EDGE, channels), F32), shape((EDGE, channels), F32),
         shape((taps, channels), F32), shape((1, channels), F32), shape((rows, heads), BF16),
         shape((rows, both), F32), shape((EDGE, heads), F32)],
        [pltpu.VMEM((length + EDGE, channels), F32), pltpu.VMEM((length + EDGE, channels), F32),
         pltpu.VMEM((channels, states), BF16), pltpu.VMEM((heads, LANES), F32)],
        2 * rows * channels * states * 3,
        (value_pre, value_pre, value_edge, value_kernel, value_bias, xs, xdt, xw, g, dy, dv, bcs, step_pre,
         dt, cum, ab, hin0, pre, carry, hin_low, ds0, post, back, dec, dbc_intra, skip_row, skip_gain,
         step_bias, log_rate),
        2 * rows * channels,
    )


def shifted(block, axis, distance):
    devices = range(lax.axis_size(axis))
    route = [(i - distance, i) for i in devices if i - distance in devices]
    return lax.ppermute(block, axis, route)


def regroup(block):
    members = block.shape[0]
    count = lax.axis_size("seq")
    groups = [list(range(i, i + members)) for i in range(0, count, members)]
    return lax.all_to_all(block, "seq", 0, 0, axis_index_groups=groups, tiled=True)


def carried(part, decay, hops, distance):
    carry = shifted(part, "seq", distance)
    for _ in range(hops - 1):
        leaving = decay * carry.astype(F32) + part.astype(F32)
        carry = shifted(leaving.astype(BF16), "seq", distance)
    return carry


def depthwise(padded, kernel, offset, length):
    summed = offset + kernel[0] * padded[0:length]
    for tap_index in range(1, kernel.shape[0]):
        summed = summed + kernel[tap_index] * padded[tap_index : tap_index + length]
    return summed


def depthwise_back(extended, kernel, length):
    margin = kernel.shape[0] - 1
    summed = kernel[0] * extended[margin : margin + length]
    for k in range(1, kernel.shape[0]):
        summed = summed + kernel[k] * extended[margin - k : margin - k + length]
    return summed


def kernel_sums(padded, pre_grad, length, taps):
    return jnp.stack([jnp.sum(pre_grad * padded[k : k + length], axis=0) for k in range(taps)])


def summed_low(part, dim):
    low = part.astype(BF16)
    return lax.psum_scatter(low, "seq", scatter_dimension=dim, tiled=True).astype(F32)


def local(
    tokens,
    cotangent,
    norm_gain,
    gate_matrix,
    value_matrix,
    state_matrix,
    step_matrix,
    value_kernel,
    value_bias,
    state_kernel,
    state_bias,
    step_bias,
    log_rate,
    skip_gain,
    gate_gain,
    output_matrix,
):
    seq_count, length, share = tokens.shape
    hops = lax.axis_size("seq") // seq_count - 1
    width, channels = gate_matrix.shape
    heads = step_bias.shape[0]
    wide = channels // heads
    both = state_matrix.shape[1]
    taps = value_kernel.shape[0]
    rows = seq_count * length
    head_count = lax.axis_size("head")
    head_rank = lax.axis_index("head")
    inner = channels * head_count
    row = lambda v: v.reshape(1, -1)

    whole_in = lax.all_gather(regroup(tokens), "head", axis=2, tiled=True).reshape(rows, width)
    flat_cot = lax.all_gather(regroup(cotangent), "head", axis=2, tiled=True).reshape(rows, width)
    plain = whole_in.astype(F32)
    rstd = lax.rsqrt(jnp.mean(plain * plain, axis=-1, keepdims=True) + EPSILON)
    normal_in = (plain * rstd * norm_gain).astype(BF16)
    state_pre = dot(normal_in, state_matrix)
    step_pre = dot(normal_in, step_matrix)
    value_pre = dot(normal_in, value_matrix)
    gate_pre = dot(normal_in, gate_matrix)

    edge = shifted(
        jnp.concatenate([value_pre[rows - EDGE :], state_pre[rows - EDGE :]], axis=1), "seq", seq_count
    )
    value_edge, state_edge = edge[:, :channels], edge[:, channels:]
    xs, xdt, xw, bcs, dt, cum, cumt, hin0, pre, dec, ending = prepare(
        value_pre, value_edge, state_pre, state_edge, step_pre, value_kernel, row(value_bias),
        state_kernel, row(state_bias), row(step_bias), row(log_rate), length,
    )
    whole_decay = jnp.repeat(pre[-1] * dec[-1], wide, axis=0)
    carry = carried(ending, whole_decay, hops, seq_count)
    y_intra = intra(bcs, xdt, cum, cumt, length)
    normed_grad = dot(flat_cot, output_matrix, NT)
    skip_row = row(jnp.repeat(skip_gain, wide))
    y, hin_low, sums = finish(
        y_intra, xs, bcs, gate_pre, normed_grad, cum, hin0, pre, carry, skip_row, row(gate_gain), length
    )
    sums = lax.psum(sums, "head")
    normed, part, dy, dz, dv, ab, ds0, post, starting, gate_gain_part = turn(
        y, gate_pre, normed_grad, xs, bcs, cum, sums, row(gate_gain), output_matrix, dec, length, inner
    )
    back = carried(starting, whole_decay, hops, -seq_count)
    branch = lax.psum_scatter(part, "head", scatter_dimension=1, tiled=True)
    layer_out = (
        tokens.astype(F32) + regroup(branch.reshape(tokens.shape)).astype(F32)
    ).astype(BF16)
    output_partial = dot(normed, flat_cot, TN)
    gate_partial = dot(normal_in, dz, TN)
    g, dbc_intra = intra_back(bcs, xdt, dy, cum, cumt, length)
    dxr, tail, head_rows, value_kernel_part, value_bias_part, ddtr, dbc, small = finish_back(
        value_pre, value_edge, value_kernel, row(value_bias), xs, xdt, xw, g, dy, dv, bcs, step_pre, dt, cum,
        ab, hin0, pre, carry, hin_low, ds0, post, back, dec, dbc_intra, skip_row, row(skip_gain),
        row(step_bias), row(log_rate), length,
    )
    dbc = lax.psum(dbc, "head")
    state_padded = jnp.concatenate([state_edge[EDGE - taps + 1 :], state_pre], axis=0)
    state_conv = depthwise(state_padded, state_kernel, state_bias, rows)
    dpre_bc = dbc * slope(state_conv)
    after = shifted(jnp.concatenate([head_rows, dpre_bc[:EDGE]], axis=1), "seq", -seq_count)
    value_after, state_after = after[:, :channels], after[:, channels:]
    zeros = jnp.zeros_like(value_after)
    fixed = tail + depthwise_back(
        jnp.concatenate([zeros, value_after[: taps - 1]], axis=0), value_kernel, EDGE
    )
    dxr = lax.dynamic_update_slice(dxr, fixed.astype(BF16), (rows - EDGE, 0))
    dbc_low = depthwise_back(
        jnp.concatenate([dpre_bc, state_after[: taps - 1]], axis=0), state_kernel, rows
    ).astype(BF16)
    state_kernel_part = kernel_sums(state_padded, dpre_bc, rows, taps)
    state_bias_part = jnp.sum(dpre_bc, axis=0)

    column_share = both // head_count
    state_columns = lax.dynamic_slice_in_dim(dbc_low, head_rank * column_share, column_share, 1)
    matrix_columns = lax.dynamic_slice_in_dim(
        state_matrix, head_rank * column_share, column_share, 1
    )
    value_partial = dot(normal_in, dxr, TN)
    normal_partial = (
        dot(dz, gate_matrix, NT)
        + dot(dxr, value_matrix, NT)
        + dot(state_columns, matrix_columns, NT)
        + dot(ddtr, step_matrix, NT)
    )
    gain_share = lax.dynamic_slice_in_dim(norm_gain, head_rank * share, share, 0)
    own_hat = lax.dynamic_slice_in_dim(plain, head_rank * share, share, 1) * rstd
    row_total = lax.psum(
        jnp.sum(normal_partial * norm_gain * (plain * rstd), axis=-1, keepdims=True), "head"
    )
    normal_grad = lax.psum_scatter(
        normal_partial.astype(BF16), "head", scatter_dimension=1, tiled=True
    ).astype(F32)
    up = rstd * (normal_grad * gain_share - own_hat * row_total / width)
    token_grad = cotangent.astype(F32) + regroup(up.astype(BF16).reshape(tokens.shape)).astype(F32)
    norm_gain_part = jnp.sum(normal_grad * own_hat, axis=0)
    step_partial = dot(normal_in, ddtr, TN)
    own_rows = lax.dynamic_slice_in_dim(normal_in, head_rank * share, share, 1)
    state_partial = dot(own_rows, dbc_low, TN)
    gate_matrix_grad, value_matrix_grad, step_matrix_grad, output_matrix_grad = (
        summed_low(gate_partial, 0),
        summed_low(value_partial, 0),
        lax.psum_scatter(step_partial, "seq", scatter_dimension=0, tiled=True),
        summed_low(output_partial, 1),
    )
    summed = lax.psum(
        (
            state_partial,
            norm_gain_part,
            value_kernel_part,
            value_bias_part[0],
            state_kernel_part,
            state_bias_part,
            small[0],
            small[1],
            small[2],
            gate_gain_part[0],
        ),
        "seq",
    )
    return (
        layer_out,
        token_grad,
        summed[1],
        gate_matrix_grad,
        value_matrix_grad,
        summed[0],
        step_matrix_grad,
        summed[2],
        summed[3],
        summed[4],
        summed[5],
        summed[6],
        summed[7],
        summed[8],
        summed[9],
        output_matrix_grad,
    )


def solution(mesh):
    in_specs = (
        P(None, "seq", "head"),
        P(None, "seq", "head"),
        P(),
        P(None, "head"),
        P(None, "head"),
        P(),
        P(None, "head"),
        P(None, "head"),
        P("head"),
        P(),
        P(),
        P("head"),
        P("head"),
        P("head"),
        P("head"),
        P("head", None),
    )
    out_specs = (
        P(None, "seq", "head"),
        P(None, "seq", "head"),
        P("head"),
        P("seq", "head"),
        P("seq", "head"),
        P("head", None),
        P("seq", "head"),
        P(None, "head"),
        P("head"),
        P(),
        P(),
        P("head"),
        P("head"),
        P("head"),
        P("head"),
        P("head", "seq"),
    )
    return jax.shard_map(local, mesh=mesh, in_specs=in_specs, out_specs=out_specs, check_vma=False)
```

time: 833 us -> 781 us (0.938)
  Pallas kernels: 0 us -> 88.8 us
  other arithmetic: 99.9 us -> 28 us
  local copies, waits for them, and re-layouts: 78.1 us -> 13 us
  matrix products: 147 us -> 89.2 us
  waiting for transfers between devices: 383 us -> 422 us
  blocking collectives: 69.9 us -> 99.4 us
  starting transfers between devices: 29.1 us -> 18.8 us
    pallas_call x0 -> x6, Pallas kernels: none -> 88.8 us  [call(): pl.pallas_call(kernel, grid=grid, in_specs=in_specs, out_specs=out_specs,...]
    dot_general x27 -> x14, matrix products: 147 us -> 89.2 us  [dot(): lax.dot_general(a, b, dims, precision=precision, preferred_element_type=F32)]
    reshape x7 -> x0, local copies, waits for them, and re-layouts: 44.1 us -> none  [the longest x3 23.5 us: local(): x_grad.reshape(1, row_count, inner_local)]
    reduce_sum x14 -> x2, other arithmetic: 44.1 us -> 5.88 us  [the longest x1 3.59 us: local(): norm_gain_part = jnp.sum(normal_grad * own_hat, axis=0)]
    psum x1, waiting for transfers between devices: 0.01 us -> 34.1 us  [local(): dbc = lax.psum(dbc, 'head')]
    reduce_scatter x5, waiting for transfers between devices: 245 us -> 272 us  [the longest x3 265 us: summed_low(): lax.psum_scatter(low, 'seq', scatter_dimension=dim, tiled=True).astype(F32)]
    all_to_all x1 -> x2, blocking collectives: 20.2 us -> 38 us  [regroup(): lax.all_to_all(block, 'seq', 0, 0, axis_index_groups=groups, tiled=True)]
    all_to_all x3 -> x2, waiting for transfers between devices: 17.6 us -> 0.01 us  [regroup(): lax.all_to_all(block, 'seq', 0, 0, axis_index_groups=groups, tiled=True)]
  transfers between devices with their start and end apart: 19 -> 16, of which waited for: 10 -> 9; matrix products, arithmetic and copies ran while one was open for 30% -> 16% of each run, Pallas kernels for 0% -> 4%
where the time goes in v2:
time: 781 us; the launch traced here: 775 us
  waiting for transfers between devices  422 us (54%)
  blocking collectives  99.4 us (13%)
  matrix products  89.2 us (11%)
  Pallas kernels  88.8 us (11%)
  other arithmetic  28 us (4%)
  starting transfers between devices  18.8 us (2%)
  between operations  15.1 us (2%)
  local copies, waits for them, and re-layouts  13 us (2%)
    reduce_scatter x3, waiting for transfers between devices, summed_low(): lax.psum_scatter(low, 'seq', scatter_dimension=dim, tiled=True).astype(F32)  265 us
    dot_general x14, matrix products, dot(): lax.dot_general(a, b, dims, precision=precision, preferred_element_type=F32)  89.2 us
    pallas_call x6, Pallas kernels, call(): pl.pallas_call(kernel, grid=grid, in_specs=in_specs, out_specs=out_specs,...  88.8 us
    psum x1, waiting for transfers between devices, local(): lax.psum((state_partial, norm_gain_part, value_kernel_part, value_bias_pa...  75.2 us
    all_to_all x2, blocking collectives, regroup(): lax.all_to_all(block, 'seq', 0, 0, axis_index_groups=groups, tiled=True)  38 us
    psum x1, blocking collectives, local(): lax.psum((state_partial, norm_gain_part, value_kernel_part, value_bias_pa...  37.1 us
    psum x1, waiting for transfers between devices, local(): dbc = lax.psum(dbc, 'head')  34.1 us
    reduce_scatter x1, waiting for transfers between devices, local(): lax.psum_scatter(step_partial, 'seq', scatter_dimension=0, tiled=True)  21.2 us
  transfers between devices with their start and end apart: 16, of which 9 were waited for; matrix products, arithmetic and copies ran while one was open for 16% of the time, Pallas kernels for 4%

profile of v2, /device:TPU:0, one launch (start us, length us, event | category | flops | bytes accessed | tf_op | source)
XLA Modules:
  0.0 774.8 jit_solution(4988198250248624604)
XLA Ops:
  7.3 20.2 %all_to_all.20 = bf16[4,256,512]{2,1,0:T(8,128)(2,1)} all-to-all(bf16[4,256,512]{2,1,0:T(8,128)(2,1)} %param.16), channel_id=1, replica_groups={{0,4,8,12},{16,20,24,28},{1,5,9,13},{17,21,25,29},{2,6,10,14},{18,22,26..., dimensions={0} | all-to-all | bytes 2097152 | tf_op jit(solution)/shard_map/all_to_all | solution.py:541
  27.5 17.8 %all_to_all.21 = bf16[4,256,512]{2,1,0:T(8,128)(2,1)} all-to-all(bf16[4,256,512]{2,1,0:T(8,128)(2,1)} %param.17), channel_id=1, replica_groups={{0,4,8,12},{16,20,24,28},{1,5,9,13},{17,21,25,29},{2,6,10,14},{18,22,26..., dimensions={0} | all-to-all | bytes 2097152 | tf_op jit(solution)/shard_map/all_to_all | solution.py:541
  46.2 15.7 %all-gather.3.cloned.1.call-done = bf16[4,256,2048]{2,1,0:T(8,128)(2,1)} async-done(((bf16[4,256,512]{2,1,0:T(8,128)(2,1)}), bf16[4,256,2048]{2,1,0:T(8,128)(2,1)}) %all-gather.3.cloned.1.call-update) | async-done | bytes 4194320 | tf_op jit(solution)/shard_map/all_gather | solution.py:607
  87.9 15.6 %conv_and_local_states.1 = (bf16[1024,1024]{1,0:T(8,128)(2,1)}, bf16[1024,1024]{1,0:T(8,128)(2,1)}, bf16[1024,1024]{1,0:T(8,128)(2,1)}, bf16[1024,256]{1,0:T(8,1...) custom-call(f32[1024,1024]{1,0:T(8,128)} %copy-done.2, ...), custom_call_target="tpu_custom_call" | custom-call | flops 268435456 | bytes 20055168 | tf_op jit(solution)/shard_map/conv_and_local_states/pallas_call | solution.py:74
  105.6 10.0 %fusion.37.dn.dn_r = f32[1024,1024]{1,0:T(8,128)} fusion(bf16[1024,2048]{1,0:T(8,128)(2,1)} %bitcast.94, bf16[1024,2048]{1,0:T(8,128)(2,1)} %wo.1), kind=kOutput, calls=%fused_computation.72 | convolution fusion | flops 4294967296 | bytes 12582912 | tf_op jit(solution)/shard_map/dot_general | solution.py:22
  122.9 10.3 %across_blocks.1 = (f32[1024,1024]{1,0:T(8,128)}, bf16[4,1024,128]{2,1,0:T(8,128)(2,1)}, f32[1024,2]{1,0:T(8,128)}) custom-call(f32[1024,1024]{1,0:T(8,128)} %within_blocks.1.yi, bf16[1024,1024]{1,0:T(8,128)(2,1)} %get-tuple-element.54.xs_r, bf16[1024,256]{1,0:T(8,128)(2,1)} %get-tuple-element.50.bcs_r, f32[1024,1024]{1,0:T(8,128)} %fusion.36.z.z_r, ...), custom_call_target="tpu_custom_call" | custom-call | flops 268435456 | bytes 22921216 | tf_op jit(solution)/shard_map/across_blocks/pallas_call | solution.py:74
  133.2 17.5 %psum.91.sums_r = f32[1024,2]{1,0:T(8,128)} all-reduce(f32[1024,2]{1,0:T(8,128)} %get-tuple-element.59), channel_id=1, replica_groups=mesh['seq'=8,'head'=4] {'head'}, use_global_device_ids=true, to_apply=%region_1.0 | all-reduce | flops 2048 | bytes 16384 | tf_op jit(solution)/shard_map/psum | solution.py:633
  150.7 18.7 %gate_and_turn.1 = (bf16[1024,1024]{1,0:T(8,128)(2,1)}, bf16[1024,2048]{1,0:T(8,128)(2,1)}, bf16[1024,1024]{1,0:T(8,128)(2,1)}, bf16[1024,1024]{1,0:T(8,128)(2,1...) custom-call(f32[1024,1024]{1,0:T(8,128)} %get-tuple-element.58.y_r, ...), custom_call_target="tpu_custom_call" | custom-call | flops 4563402752 | bytes 34619392 | tf_op jit(solution)/shard_map/gate_and_turn/pallas_call | solution.py:74
  170.6 12.4 %within_blocks_back.1 = (f32[1024,1024]{1,0:T(8,128)}, f32[1024,256]{1,0:T(8,128)}) custom-call(bf16[1024,256]{1,0:T(8,128)(2,1)} %get-tuple-element.50.bcs_r, bf16[1024,1024]{1,0:T(8,128)(2,1)} %get-tuple-element.51.xdt_r, bf16[1024,1024]{1,0:T(8,128)(2,1)} %get-tuple-element.64.dy_r, f32[1024,16]{1,0:T(8,128)} %get-tuple-element.52.cum_r, ...), custom_call_target="tpu_custom_call" | custom-call | flops 4294967296 | bytes 10092544 | tf_op jit(solution)/shard_map/within_blocks_back/pallas_call | solution.py:74
  187.0 25.2 %across_blocks_back.1 = (bf16[1024,1024]{1,0:T(8,128)(2,1)}, f32[8,1024]{1,0:T(8,128)}, f32[8,1024]{1,0:T(8,128)}, f32[4,1024]{1,0:T(4,128)}, f32[1,1024]{1,0:T(...) custom-call(f32[1024,1024]{1,0:T(8,128)} %copy-done.2, f32[1024,1024]{1,0:T(8,128)} %copy-done.2, ...), custom_call_target="tpu_custom_call" | custom-call | flops 805306368 | bytes 34157248 | tf_op jit(solution)/shard_map/across_blocks_back/pallas_call | solution.py:74
  213.0 34.1 %all-reduce.5.cloned.1.call-done = f32[1024,256]{1,0:T(8,128)} async-done(((f32[1024,256]{1,0:T(8,128)}), f32[1024,256]{1,0:T(8,128)}) %all-reduce.5.cloned.1.call-update) | async-done | bytes 1048592 | tf_op jit(solution)/shard_map/psum | solution.py:650
  250.9 10.9 %fusion.38 = f32[1024,2048]{1,0:T(8,128)} fusion(bf16[1024,1024]{1,0:T(8,128)(2,1)} %get-tuple-element.62, bf16[2048,1024]{1,0:T(8,128)(2,1)} %param.19), kind=kOutput, calls=%fused_computation.73 | convolution fusion | flops 4294967296 | bytes 14680064 | tf_op jit(solution)/shard_map/dot_general | solution.py:22
  267.9 6.9 fusion.39
  274.8 11.9 %multiply_reduce_fusion = (f32[1024]{0:T(1024)S(1)}, bf16[1024,2048]{1,0:T(8,128)(2,1)}) fusion(f32[2048]{0:T(1024)S(1)} %copy-done.16, f32[1024]{0:T(1024)S(1)} %bitcast.64, bf16[4,256,2048]{2,1,0:T(8,128)(2,1)S(1)} %copy-done.4, bf16[1024,16]{1,0:T(8,128)(2,1)S(1)} %copy-done.12, bf16[2048,16]{0,1:T(8,128)(2,1)S(1)} %copy-done.15, f32[1024,2048]{1,0:T(8,128)} %fusion.17, ...), kind=kOutput, calls=%fused_computation | convolution fusion | flops 85982208 | bytes 33669120 | tf_op jit(solution)/shard_map/dot_general | solution.py:22
  288.3 8.4 %convolution_convert_fusion.2 = bf16[2048,1024]{1,0:T(8,128)(2,1)} fusion(bf16[1024,2048]{1,0:T(8,128)(2,1)} %copy-done.5, bf16[1024,1024]{1,0:T(8,128)(2,1)S(1)} %copy-done.29), kind=kOutput, calls=%fused_computation.6 | convolution fusion | flops 4297064448 | bytes 10485760 | tf_op jit(solution)/shard_map/dot_general | solution.py:22
  298.3 8.3 %convolution_convert_fusion = bf16[1024,2048]{1,0:T(8,128)(2,1)} fusion(bf16[1024,1024]{1,0:T(8,128)(2,1)S(1)} %copy-done.28, bf16[1024,2048]{1,0:T(8,128)(2,1)} %bitcast.95), kind=kOutput, calls=%fused_computation.4 | convolution fusion | flops 4297064448 | bytes 10485760 | tf_op jit(solution)/shard_map/dot_general | solution.py:22
  308.3 8.4 %convolution_convert_fusion.1 = bf16[2048,1024]{1,0:T(8,128)(2,1)} fusion(bf16[1024,2048]{1,0:T(8,128)(2,1)} %copy-done.5, bf16[1024,1024]{1,0:T(8,128)(2,1)S(1)} %copy-done.32), kind=kOutput, calls=%fused_computation.5 | convolution fusion | flops 4297064448 | bytes 10485760 | tf_op jit(solution)/shard_map/dot_general | solution.py:22
  334.1 7.5 reduce-scatter.9.cloned.1.call-done
  356.6 85.3 %reduce-scatter.11.cloned.1.call-done = bf16[256,1024]{1,0:T(8,128)(2,1)} async-done(((bf16[2048,1024]{1,0:T(8,128)(2,1)}), bf16[256,1024]{1,0:T(8,128)(2,1)}) %reduce-scatter.11.cloned.1.call-update) | async-done | bytes 524304 | tf_op jit(solution)/shard_map/reduce_scatter | solution.py:573
  444.0 89.8 %reduce-scatter.17.cloned.1.call-done = bf16[1024,256]{1,0:T(8,128)(2,1)} async-done(((bf16[1024,2048]{1,0:T(8,128)(2,1)}), bf16[1024,256]{1,0:T(8,128)(2,1)}) %reduce-scatter.17.cloned.1.call-update) | async-done | bytes 524304 | tf_op jit(solution)/shard_map/reduce_scatter | solution.py:573
  535.8 89.6 %reduce-scatter.13.cloned.1.call-done = bf16[256,1024]{1,0:T(8,128)(2,1)} async-done(((bf16[2048,1024]{1,0:T(8,128)(2,1)}), bf16[256,1024]{1,0:T(8,128)(2,1)}) %reduce-scatter.13.cloned.1.call-update) | async-done | bytes 524304 | tf_op jit(solution)/shard_map/reduce_scatter | solution.py:573
  627.6 37.1 %all-reduce.1 = (f32[512]{0:T(512)}, f32[4,1024]{1,0:T(4,128)}, f32[1024]{0:T(1024)}, f32[4,256]{1,0:T(4,128)}, f32[256]{0:T(256)}, /*index=5*/f32[16]{0:T(128)}, f32[16]{0:T(128)}, f32[16]{0:T(128)}, f32[1024]{0:T(1024)}) all-reduce(f32[512]{0:T(512)S(1)} %get-tuple-element.99, ...), channel_id=1, replica_groups=mesh['seq'=8,'head'=4] {'seq'}, use_global_device_ids=true, to_apply=%region_8.0 | all-reduce | flops 7984 | bytes 63872 | tf_op jit(solution)/shard_map/psum | solution.py:699
  669.2 21.2 %reduce-scatter.15.cloned.1.call-done = f32[256,16]{0,1:T(8,128)} async-done(((f32[2048,16]{0,1:T(8,128)}), f32[256,16]{0,1:T(8,128)}) %reduce-scatter.15.cloned.1.call-update) | async-done | bytes 16400 | tf_op jit(solution)/shard_map/reduce_scatter | solution.py:696
  690.4 75.2 %all-reduce.7.cloned.1.call-done = f32[512,256]{1,0:T(8,128)} async-done(((f32[512,256]{1,0:T(8,128)}), f32[512,256]{1,0:T(8,128)}) %all-reduce.7.cloned.1.call-update) | async-done | bytes 524304 | tf_op jit(solution)/shard_map/psum | solution.py:699
  (141 shorter events, 101.8 us)
Async XLA Ops:
  7.2 64.9 %copy-start = (bf16[2048,256]{1,0:T(8,128)(2,1)S(1)}, bf16[2048,256]{1,0:T(8,128)(2,1)}, u32[]{:S(2)}) copy-start(bf16[2048,256]{1,0:T(8,128)(2,1)} %param.21) | copy-start | bytes 3145732
  7.2 38.2 %copy-start.24 = (f32[16]{0:T(128)S(1)}, f32[16]{0:T(128)}, u32[]{:S(2)}) copy-start(f32[16]{0:T(128)} %param.29) | copy-start | bytes 196
  7.2 54.7 %all-gather.3.cloned.1.call-start = ((), (), s32[]{:S(2)}) async-start(), calls=%async_computation.10 | async-start | bytes 5242880 | tf_op jit(solution)/shard_map/all_gather | solution.py:607
  27.4 37.7 %copy-start.16 = (f32[2048]{0:T(1024)S(1)}, f32[2048]{0:T(1024)}, u32[]{:S(2)}) copy-start(f32[2048]{0:T(1024)} %param.18) | copy-start | bytes 24580
  27.5 78.1 %all-gather.5.cloned.1.call-start = ((), (), s32[]{:S(2)}) async-start(), calls=%async_computation.11 | async-start | bytes 5242880 | tf_op jit(solution)/shard_map/all_gather | solution.py:608
  45.4 201.7 %all-reduce.5.cloned.1.call-start = ((), (), s32[]{:S(2)}) async-start(), calls=%async_computation.13 | async-start | bytes 2097152 | tf_op jit(solution)/shard_map/psum | solution.py:650
  73.4 13.2 %collective-permute-start = (f32[8,1280]{1,0:T(8,128)S(1)}, f32[8,1280]{1,0:T(8,128)S(1)}, u32[]{:S(2)}, u32[]{:S(2)}) collective-permute-start(f32[8,1280]{1,0:T(8,128)S(1)} %pad_maximum_fusion.2), channel_id=1, source_target_pairs={{0,16},{4,20},{8,24},{12,28},{1,17},{5,21},{9,25},{13,29},{2,18},{... | collective-permute-start | bytes 122888 | tf_op jit(solution)/shard_map/ppermute | solution.py:534
  103.5 18.7 %collective-permute-start.1 = (bf16[1024,128]{1,0:T(8,128)(2,1)}, bf16[1024,128]{1,0:T(8,128)(2,1)S(1)}, u32[]{:S(2)}, u32[]{:S(2)}) collective-permute-start(bf16[1024,128]{1,0:T(8,128)(2,1)} %get-tuple-element.57), channel_id=1, source_target_pairs={{0,16},{4,20},{8,24},{12,28},{1,17},{5,21},{9,25},{13,29},{2,18},{... | collective-permute-start | bytes 786440 | tf_op jit(solution)/shard_map/ppermute | solution.py:534
  169.3 16.9 %collective-permute-start.2 = (bf16[1024,128]{1,0:T(8,128)(2,1)}, bf16[1024,128]{1,0:T(8,128)(2,1)S(1)}, u32[]{:S(2)}, u32[]{:S(2)}) collective-permute-start(bf16[1024,128]{1,0:T(8,128)(2,1)} %get-tuple-element.72), channel_id=1, source_target_pairs={{16,0},{20,4},{24,8},{28,12},{17,1},{21,5},{25,9},{29,13},{18,2},{... | collective-permute-start | bytes 786440 | tf_op jit(solution)/shard_map/ppermute | solution.py:534
  212.3 104.5 %reduce-scatter.7.cloned.1.call-start = ((), (), s32[]{:S(2)}) async-start(), calls=%async_computation.12 | async-start | bytes 5242880 | tf_op jit(solution)/shard_map/reduce_scatter | solution.py:638
  212.8 128.7 %reduce-scatter.9.cloned.1.call-start = ((), (), s32[]{:S(2)}) async-start(), calls=%async_computation.14 | async-start | bytes 5242880 | tf_op jit(solution)/shard_map/reduce_scatter | solution.py:684
  249.4 12.4 %collective-permute-start.3 = (f32[8,1280]{1,0:T(8,128)S(1)}, f32[8,1280]{1,0:T(8,128)S(1)}, u32[]{:S(2)}, u32[]{:S(2)}) collective-permute-start(f32[8,1280]{1,0:T(8,128)S(1)} %pad_maximum_fusion.3), channel_id=1, source_target_pairs={{16,0},{20,4},{24,8},{28,12},{17,1},{21,5},{25,9},{29,13},{18,2},{... | collective-permute-start | bytes 122888 | tf_op jit(solution)/shard_map/ppermute | solution.py:534
  286.8 155.1 %reduce-scatter.11.cloned.1.call-start = ((), (), s32[]{:S(2)}) async-start(), calls=%async_computation.15 | async-start | bytes 4718592 | tf_op jit(solution)/shard_map/reduce_scatter | solution.py:573
  296.8 237.0 %reduce-scatter.17.cloned.1.call-start = ((), (), s32[]{:S(2)}) async-start(), calls=%async_computation.19 | async-start | bytes 4718592 | tf_op jit(solution)/shard_map/reduce_scatter | solution.py:573
  306.6 318.8 %reduce-scatter.13.cloned.1.call-start = ((), (), s32[]{:S(2)}) async-start(), calls=%async_computation.16 | async-start | bytes 4718592 | tf_op jit(solution)/shard_map/reduce_scatter | solution.py:573
  316.8 28.4 %all-to-all-start.2 = ((bf16[4,256,512]{2,1,0:T(8,128)(2,1)}), bf16[4,256,512]{2,1,0:T(8,128)(2,1)S(1)}, u32[]{:S(2)}, u32[]{:S(2)}) async-start(bf16[4,256,512]{2,1,0:T(8,128)(2,1)} %bitcast.62), calls=%async_computation.3 | async-start | bytes 2097152 | tf_op jit(solution)/shard_map/all_to_all | solution.py:541
  345.2 320.8 %all-to-all-start.3 = ((bf16[4,256,512]{2,1,0:T(8,128)(2,1)}), bf16[4,256,512]{2,1,0:T(8,128)(2,1)}, u32[]{:S(2)}, u32[]{:S(2)}) async-start(bf16[4,256,512]{2,1,0:T(8,128)(2,1)} %bitcast.17), calls=%async_computation.5 | async-start | bytes 2097152 | tf_op jit(solution)/shard_map/all_to_all | solution.py:541
  349.6 340.8 %reduce-scatter.15.cloned.1.call-start = ((), (), s32[]{:S(2)}) async-start(), calls=%async_computation.18 | async-start | bytes 147456 | tf_op jit(solution)/shard_map/reduce_scatter | solution.py:696
  353.1 274.5 %copy-start.20 = (f32[4,1024]{1,0:T(4,128)S(1)}, f32[4,1024]{1,0:T(4,128)}, u32[]{:S(2)}) copy-start(f32[4,1024]{1,0:T(4,128)} %get-tuple-element.79) | copy-start | bytes 49156
  353.1 274.5 %copy-start.22 = (f32[1,1024]{1,0:T(1,128)S(1)}, f32[1,1024]{1,0:T(1,128)}, u32[]{:S(2)}) copy-start(f32[1,1024]{1,0:T(1,128)} %get-tuple-element.82) | copy-start | bytes 12292
  353.1 274.5 %copy-start.23 = (f32[1,1024]{1,0:T(1,128)S(1)}, f32[1,1024]{1,0:T(1,128)}, u32[]{:S(2)}) copy-start(f32[1,1024]{1,0:T(1,128)} %get-tuple-element.80) | copy-start | bytes 12292
  353.1 311.5 %copy-start.8 = (bf16[4,256,512]{2,1,0:T(8,128)(2,1)S(1)}, bf16[4,256,512]{2,1,0:T(8,128)(2,1)}, u32[]{:S(2)}) copy-start(bf16[4,256,512]{2,1,0:T(8,128)(2,1)} %param.16) | copy-start | bytes 3145732
  353.2 412.4 %all-reduce.7.cloned.1.call-start = ((), (), s32[]{:S(2)}) async-start(), calls=%async_computation.17 | async-start | bytes 1048576 | tf_op jit(solution)/shard_map/psum | solution.py:699
  627.6 139.9 %copy-start.1 = (bf16[2048,256]{1,0:T(8,128)(2,1)S(1)}, bf16[2048,256]{1,0:T(8,128)(2,1)}, u32[]{:S(2)}) copy-start(bf16[2048,256]{1,0:T(8,128)(2,1)} %param.21) | copy-start | bytes 3145732
  (25 other events, 241.7 us)
Sparse Core Ops, SparseCore 0:
  27.6 34.2 all-gather.2
  63.5 34.4 all-gather.4
  212.4 34.6 all-reduce.4
  249.6 44.8 reduce-scatter.6
  296.9 44.6 reduce-scatter.8
  345.5 96.3 reduce-scatter.10
  445.5 88.2 reduce-scatter.16
  537.8 87.6 reduce-scatter.12
  629.4 60.9 reduce-scatter.14
  694.2 71.3 all-reduce.6

commit v3 on v2

--- a/solution.py
+++ b/solution.py
@@ -273,7 +273,7 @@
     )
 
 
-def turn(y, gate_pre, normed_grad, xs, bcs, cum, sums, gate_gain, output_matrix, dec, length, inner):
+def turn(y, gate_pre, normed_grad, xs, bcs, cum, sums, gate_gain, output_matrix, dec, length, shares):
     rows, channels = xs.shape
     heads = cum.shape[1]
     both = bcs.shape[1]
@@ -281,6 +281,8 @@
     wide = channels // heads
     count = rows // length
     width = output_matrix.shape[1]
+    share = width // shares
+    inner = channels * shares
 
     def kernel(y_r, z_r, dn_r, xs_r, bcs_r, cum_r, sums_r, gain, wo, dec_r,
                normed_o, part_o, dy_o, dz_o, dv_o, ab_o, ds_o, post_o, start_o, ggain_o,
@@ -316,7 +318,9 @@
         picker = head_picker(channels, heads)
         ab_o[:, :heads] = dot_split(prod_a[...], picker)
         ab_o[:, heads:] = dot_split(prod_b[...], picker)
-        part_o[...] = dot(normed_o[...], wo[...]).astype(BF16)
+        for q in range(shares):
+            at = slice(q * share, (q + 1) * share)
+            part_o[q] = dot(normed_o[...], wo[:, at]).astype(BF16)
         dhin = dot(dv_o[...], bcs_r[:, states:], TN)
         ds_o[0] = state[...]
         post_o[0] = behind[...]
@@ -334,10 +338,10 @@
         kernel, "gate_and_turn", (count,),
         [tokens(channels), tokens(channels), tokens(channels), tokens(channels), tokens(both),
          tokens(heads), tokens(2), whole(1, channels), whole(channels, width), per(heads, LANES)],
-        [tokens(channels), tokens(width), tokens(channels), tokens(channels), tokens(channels),
-         tokens(2 * heads), per(channels, states), per(heads, LANES), whole(channels, states),
+        [tokens(channels), pl.BlockSpec((shares, length, share), lambda i: (0, last - i, 0)),
+         tokens(channels), tokens(channels), tokens(channels), tokens(2 * heads), per(channels, states), per(heads, LANES), whole(channels, states),
          whole(1, channels)],
-        [shape((rows, channels), BF16), shape((rows, width), BF16), shape((rows, channels), BF16),
+        [shape((rows, channels), BF16), shape((shares, rows, share), BF16), shape((rows, channels), BF16),
          shape((rows, channels), BF16), shape((rows, channels), BF16), shape((rows, 2 * heads), F32),
          shape((count, channels, states), F32), shape((count, heads, LANES), F32),
          shape((channels, states), BF16), shape((1, channels), F32)],
@@ -528,6 +532,587 @@
     )
 
 
+def halves(normal_in, grad, outer):
+    rows, width = normal_in.shape
+    channels = grad.shape[1]
+    strip = width // (2 * outer)
+
+    def kernel(xn, grad_r, keep_o, give_o):
+        side = lax.rem(lax.axis_index("seq"), 2)
+        product = dot(xn[...], grad_r[...], TN).astype(BF16)
+
+        @pl.when(side == 0)
+        def _():
+            keep_o[0] = product[:strip]
+            give_o[0] = product[strip:]
+
+        @pl.when(side == 1)
+        def _():
+            keep_o[0] = product[strip:]
+            give_o[0] = product[:strip]
+
+    out = pl.BlockSpec((1, strip, channels), lambda i: (i, 0, 0))
+    return call(
+        kernel, "gate_strips", (outer,),
+        [pl.BlockSpec((rows, 2 * strip), lambda i: (0, i)),
+         pl.BlockSpec((rows, channels), lambda i: (0, 0))],
+        [out, out], [shape((outer, strip, channels), BF16)] * 2, [], 2 * rows * width * channels,
+        (normal_in, grad),
+    )
+
+
+def remote(src, dst, send, recv, seq, head):
+    return pltpu.make_async_remote_copy(
+        src_ref=src, dst_ref=dst, send_sem=send, recv_sem=recv, device_id=(seq, head),
+        device_id_type=pl.DeviceIdType.MESH,
+    )
+
+
+def greet(seq, head, seq_size, head_size):
+    barrier = pltpu.get_barrier_semaphore()
+    for d in range(1, seq_size):
+        pl.semaphore_signal(
+            barrier, inc=1, device_id=(lax.rem(seq + d, seq_size), head),
+            device_id_type=pl.DeviceIdType.MESH,
+        )
+    for d in range(1, head_size):
+        pl.semaphore_signal(
+            barrier, inc=1, device_id=(seq, lax.rem(head + d, head_size)),
+            device_id_type=pl.DeviceIdType.MESH,
+        )
+    pl.semaphore_wait(barrier, seq_size - 1 + head_size - 1)
+
+
+def closing(normal_in, dz, dxr, tail, head_rows, gate_matrix, value_matrix, state_matrix, step_matrix,
+            value_kernel, state_kernel, state_bias, state_pre, state_edge, dbc, ddtr, vectors, small,
+            part, mine, rstd, gain_share, gate_half, length, seq_size, head_size):
+    rows, width = normal_in.shape
+    channels = dz.shape[1]
+    heads = ddtr.shape[1]
+    both = dbc.shape[1]
+    share = mine.shape[1]
+    taps = value_kernel.shape[0]
+    members = rows // length
+    outer = seq_size // 2
+    half_heads = head_size // 2
+    strip = width // seq_size
+    chunk = rows // head_size
+    per = head_size // members
+    piece = share // seq_size
+    piece_type = BF16 if piece % 16 == 0 else F32
+    packed = channels + both + LANES
+    groups = seq_size // members
+
+    def kernel(xn, dz_r, dxr_h, tail_r, head_r, gate_h, value_h, state_m, step_m, vk, sk, sb, bc_h,
+               bc_edge, dbc_h, ddtr_r, vec, small_r, part_h, mine_r, rstd_r, gain, half_h,
+               gate_o, value_o, state_o, step_o, vec_o, norm_o, up_o, branch_o,
+               dxr_r, duo, xrecv, zrecv, gown, grecv, weights, weight, csend, cown, crecv, yrecv, rsend,
+               rrecv, up, nsend, nrecv,
+               pown, precv, pyrecv, drecv, dsum, ext, hrecv, hbrecv, low, spart, srecv, ssum, sall,
+               tsend, trecv, vsend, vrecv,
+               xs_sem, xr_sem, zs_sem, zr_sem, cs_sem, cr_sem, ys_sem, yr_sem, rs_sem, rr_sem,
+               us_sem, ur_sem, ns_sem, nr_sem, ps_sem, pr_sem, pys_sem, pyr_sem, ds_sem, dr_sem,
+               as_sem, ar_sem, h_sem, hb_sem, ss_sem, sr_sem, sas_sem, sar_sem, ts_sem, tr_sem,
+               vs_sem, vr_sem, bs_sem, br_sem, gs_sem, gr_sem, w_sem, copy_sem):
+        seq, head = lax.axis_index("seq"), lax.axis_index("head")
+        place, side = seq // 2, lax.rem(seq, 2)
+        lane, core = head // 2, lax.rem(head, 2)
+        group, member = seq // members, lax.rem(seq, members)
+        base = seq - member
+        load_dxr = pltpu.make_async_copy(dxr_h, dxr_r, copy_sem.at[0])
+        load_dxr.start()
+        load_bc = pltpu.make_async_copy(bc_h, low.at[pl.ds(EDGE, rows)], copy_sem.at[1 + half_heads])
+        load_bc.start()
+        low[0:EDGE] = bc_edge[...]
+
+        def outer_at(k):
+            return lax.rem(place + 1 + k, outer)
+
+        def lane_at(k):
+            return lax.rem(lane + 1 + k, half_heads)
+
+        def seq_at(d):
+            return lax.rem(seq + d, seq_size)
+
+        def head_at(d):
+            return lax.rem(head + d, head_size)
+
+        loads = [
+            pltpu.make_async_copy(part_h.at[2 * lane_at(k) + core], pown.at[k], copy_sem.at[1 + k])
+            for k in range(half_heads)
+        ]
+        for load in loads:
+            load.start()
+        own_rows = pl.ds(pl.multiple_of(head * chunk, chunk), chunk)
+        load_dbc = pltpu.make_async_copy(
+            dbc_h.at[own_rows], dsum.at[own_rows], copy_sem.at[2 + half_heads]
+        )
+        load_dbc.start()
+        load_half = pltpu.make_async_copy(half_h.at[place], gown, copy_sem.at[3 + half_heads])
+        load_half.start()
+        greet(seq, head, seq_size, head_size)
+
+        def cross(k):
+            return remote(duo.at[k, 1 - side], xrecv.at[k], xs_sem.at[k], xr_sem.at[k],
+                          2 * place + 1 - side, head)
+
+        def along(k):
+            return remote(duo.at[k, side], zrecv.at[k], zs_sem.at[k], zr_sem.at[k],
+                          2 * outer_at(k) + side, head)
+
+        def along_gate(k):
+            return remote(half_h.at[outer_at(k)], grecv.at[k], gs_sem.at[k], gr_sem.at[k],
+                          2 * outer_at(k) + side, head)
+
+        def edge_back(src, dst, sems):
+            return remote(src, dst, sems.at[0], sems.at[1], seq - members, head)
+
+        def part_core(k):
+            return remote(part_h.at[2 * lane_at(k) + 1 - core], precv.at[k], ps_sem.at[k], pr_sem.at[k],
+                          seq, 2 * lane + 1 - core)
+
+        def part_lane(k):
+            return remote(pown.at[k], pyrecv.at[k], pys_sem.at[k], pyr_sem.at[k],
+                          seq, 2 * lane_at(k) + core)
+
+        def rows_of(c):
+            return pl.ds(pl.multiple_of(c * chunk, chunk), chunk)
+
+        def basis_sum(d):
+            return remote(dbc_h.at[rows_of(head_at(d))], drecv.at[d - 1], ds_sem.at[d - 1],
+                          dr_sem.at[d - 1], seq, head_at(d))
+
+        def basis_share(d):
+            at = rows_of(head)
+            return remote(dsum.at[at], dsum.at[at], as_sem.at[d - 1], ar_sem.at[d - 1], seq, head_at(d))
+
+        @pl.when(group > 0)
+        def _():
+            edge_back(head_r, hrecv, h_sem).start()
+
+        for d in range(1, head_size):
+            basis_sum(d).start()
+        for k in range(half_heads):
+            part_core(k).start()
+
+        for k in range(outer - 1):
+            along_gate(k).start()
+
+        load_dxr.wait()
+        ext[...] = jnp.zeros_like(ext)
+
+        @pl.when(group < groups - 1)
+        def _():
+            remote(head_r, hrecv, h_sem.at[0], h_sem.at[1], seq, head).wait_recv()
+            ext[EDGE:] = hrecv[...]
+
+        fixed = tail_r[...]
+        for k in range(taps):
+            fixed = fixed + vk[k : k + 1] * ext[pl.ds(taps - 1 - k, EDGE)]
+        last = dxr_r[rows - 2 * EDGE :].astype(F32)
+        dxr_r[rows - 2 * EDGE :] = jnp.concatenate([last[:EDGE], fixed], axis=0).astype(BF16)
+
+        def multiply(k, _):
+            at = pl.ds(pl.multiple_of(outer_at(k) * 2 * strip, 2 * strip), 2 * strip)
+            product = dot(xn[:, at], dxr_r[...], TN).astype(BF16)
+            duo[k, 0] = product[:strip]
+            duo[k, 1] = product[strip:]
+            cross(k).start()
+            return 0
+
+        lax.fori_loop(0, outer, multiply, 0)
+
+        load_dbc.wait()
+        total = dsum[own_rows]
+        for d in range(1, head_size):
+            basis_sum(d).wait_recv()
+            total = total + drecv[d - 1]
+        dsum[own_rows] = total
+        for d in range(1, head_size):
+            basis_share(d).start()
+
+        tsend_v = dot(ddtr_r[...], xn[...], TN)
+        for o in range(outer):
+            tsend[o] = tsend_v[:, o * 2 * strip : (o + 1) * 2 * strip]
+
+        def step_piece(d):
+            return remote(tsend.at[seq_at(d) // 2], trecv.at[d - 1], ts_sem.at[d - 1], tr_sem.at[d - 1],
+                          seq_at(d), head)
+
+        for d in range(1, seq_size):
+            step_piece(d).start()
+
+        def arrived(k, send=True):
+            cross(k).wait_recv()
+            duo[k, side] = (duo[k, side].astype(F32) + xrecv[k].astype(F32)).astype(BF16)
+            if send:
+                along(k).start()
+
+        def arrived_loop(first, last):
+            def one(k, _):
+                arrived(k)
+                return 0
+
+            lax.fori_loop(first, last, one, 0)
+
+        for k in range(half_heads):
+            loads[k].wait()
+            part_core(k).wait_recv()
+            for r in range(members):
+                at = slice(r * length, (r + 1) * length)
+                pown[k, at] = (pown[k, at].astype(F32) + precv[k, at].astype(F32)).astype(BF16)
+            if k < half_heads - 1:
+                part_lane(k).start()
+
+        for d in range(1, head_size):
+            at = rows_of(head_at(d))
+            remote(dsum.at[at], dsum.at[at], as_sem.at[d - 1], ar_sem.at[head_size - 1 - d],
+                   seq, head).wait_recv()
+
+        start = EDGE - taps + 1
+        load_bc.wait()
+        pre_bc = sb[...]
+        for k in range(taps):
+            pre_bc = pre_bc + sk[k : k + 1] * low[pl.ds(start + k, rows)]
+        dpre = dsum[...] * slope(pre_bc)
+        vsend[...] = jnp.zeros_like(vsend)
+        vsend[:, :channels] = vec[...]
+        vsend[:, channels + both : channels + both + heads] = small_r[...]
+        for k in range(taps):
+            vsend[k : k + 1, channels : channels + both] = jnp.sum(
+                dpre * low[pl.ds(start + k, rows)], axis=0, keepdims=True
+            )
+        vsend[taps : taps + 1, channels : channels + both] = jnp.sum(dpre, axis=0, keepdims=True)
+        low[0:rows] = dpre
+        low[rows:] = jnp.zeros((EDGE, both), F32)
+
+        @pl.when(group > 0)
+        def _():
+            edge_back(low.at[pl.ds(0, EDGE)], hbrecv, hb_sem).start()
+
+        def vector(d):
+            return remote(vsend, vrecv.at[d - 1], vs_sem.at[d - 1], vr_sem.at[d - 1], seq_at(d), head)
+
+        for d in range(1, seq_size):
+            vector(d).start()
+        arrived_loop(0, outer // 4)
+
+        @pl.when(group < groups - 1)
+        def _():
+            remote(low.at[pl.ds(0, EDGE)], hbrecv, hb_sem.at[0], hb_sem.at[1], seq, head).wait_recv()
+            low[rows:] = hbrecv[...]
+
+        dbc_v = sk[0:1] * low[pl.ds(taps - 1, rows)]
+        for k in range(1, taps):
+            dbc_v = dbc_v + sk[k : k + 1] * low[pl.ds(taps - 1 - k, rows)]
+        dbc_low = dbc_v.astype(BF16)
+        own_at = pl.ds(pl.multiple_of(head * share, share), share)
+        own_state = dot(xn[:, own_at], dbc_low, TN)
+        for s in range(seq_size):
+            spart[s] = own_state[s * piece : (s + 1) * piece].astype(piece_type)
+        for d in range(1, head_size):
+            basis_share(d).wait_send()
+        dsum[...] = dbc_low.astype(F32)
+
+        def state_piece(d):
+            return remote(spart.at[seq_at(d)], srecv.at[d - 1], ss_sem.at[d - 1], sr_sem.at[d - 1],
+                          seq_at(d), head)
+
+        for d in range(1, seq_size):
+            state_piece(d).start()
+
+        def to_core(k):
+            return remote(csend.at[k], crecv.at[k], cs_sem.at[k], cr_sem.at[k], seq, 2 * lane + 1 - core)
+
+        def to_lane(k):
+            return remote(cown.at[k], yrecv.at[k], ys_sem.at[k], yr_sem.at[k],
+                          seq, 2 * lane_at(k) + core)
+
+        def columns_of(step):
+            which = 1 - core if step < half_heads else core
+            at = (2 * lane_at(step % half_heads) + which) * share
+            return pl.ds(pl.multiple_of(at, share), share)
+
+        def fetch(step):
+            at, slot = columns_of(step), step % 2
+            return [
+                pltpu.make_async_copy(gate_h.at[at], weights.at[slot, 0], w_sem.at[slot, 0]),
+                pltpu.make_async_copy(value_h.at[at], weights.at[slot, 1], w_sem.at[slot, 1]),
+            ]
+
+        for step in range(head_size):
+            slot, at, k = step % 2, columns_of(step), step % half_heads
+            keep = csend if step < half_heads else cown
+            if step == 0:
+                for load in fetch(0):
+                    load.start()
+            if step < head_size - 1:
+                for load in fetch(step + 1):
+                    load.start()
+            for load in fetch(step):
+                load.wait()
+
+            def back_rows(c, _, slot=slot, at=at, k=k, keep=keep, first=step == 0):
+                at_rows = rows_of(c)
+                basis = jnp.where(c == head, dsum[at_rows], 0.0).astype(BF16)
+                grad = (
+                    dot(dz_r[at_rows], weights[slot, 0], NT) + dot(dxr_r[at_rows], weights[slot, 1], NT)
+                    + dot(basis, state_m[at], NT) + dot(ddtr_r[at_rows], step_m[at], NT)
+                )
+                keep[k, at_rows] = grad.astype(BF16)
+                weighed = grad * xn[at_rows, at].astype(F32)
+                total = weighed[:, :LANES] if first else weight[at_rows] + weighed[:, :LANES]
+                for q in range(1, share // LANES):
+                    total += weighed[:, q * LANES : (q + 1) * LANES]
+                weight[at_rows] = total
+                return 0
+
+            lax.fori_loop(0, head_size, back_rows, 0)
+            if step < half_heads:
+                to_core(k).start()
+            else:
+                to_core(k).wait_recv()
+
+                def add_rows(c, _, k=k):
+                    at_rows = rows_of(c)
+                    cown[k, at_rows] = (
+                        cown[k, at_rows].astype(F32) + crecv[k, at_rows].astype(F32)
+                    ).astype(BF16)
+                    return 0
+
+                lax.fori_loop(0, head_size, add_rows, 0)
+                if k < half_heads - 1:
+                    to_lane(k).start()
+            if step == 0:
+                arrived_loop(outer // 4, outer // 2)
+            if step == head_size - 2:
+                arrived_loop(outer // 2, outer - 1)
+
+        rsend[...] = dot(jnp.ones((8, LANES), F32), weight[...], NT, precision=HIGH)
+
+        def row_sums(d):
+            return remote(rsend, rrecv.at[d - 1], rs_sem.at[d - 1], rr_sem.at[d - 1], seq, head_at(d))
+
+        for d in range(1, head_size):
+            row_sums(d).start()
+
+        state_sum = spart[seq].astype(F32)
+        for d in range(1, seq_size):
+            state_piece(d).wait_recv()
+            state_sum = state_sum + srecv[d - 1].astype(F32)
+        sall[seq] = state_sum.astype(piece_type)
+
+        def state_share(d):
+            return remote(sall.at[seq], sall.at[seq], sas_sem.at[d - 1], sar_sem.at[d - 1],
+                          seq_at(d), head)
+
+        for d in range(1, seq_size):
+            state_share(d).start()
+        def give(src, out, r, sems_s, sems_r):
+            return remote(src.at[r], out.at[member], sems_s.at[r], sems_r.at[member], base + r, head)
+
+        for k in range(half_heads - 1):
+            part_lane(k).wait_recv()
+        for r in range(members):
+            at = slice(r * length, (r + 1) * length)
+            total = pown[half_heads - 1, at].astype(F32)
+            for k in range(half_heads - 1):
+                total = total + pyrecv[k, at].astype(F32)
+            precv[0, at] = total.astype(BF16)
+
+        def branch_rows(r):
+            return precv.at[0, pl.ds(r * length, length)]
+
+        for r in range(members):
+            @pl.when(r != member)
+            def _(r=r):
+                remote(branch_rows(r), branch_o.at[member], bs_sem.at[r], br_sem.at[member],
+                       base + r, head).start()
+
+            @pl.when(r == member)
+            def _(r=r):
+                pltpu.make_async_copy(branch_rows(r), branch_o.at[r], copy_sem.at[0]).start()
+
+        arrived(outer - 1, False)
+        for d in range(1, head_size):
+            row_sums(d).wait_recv()
+        sums = rsend[...]
+        for d in range(1, head_size):
+            sums = sums + rrecv[d - 1]
+        pick = (lax.broadcasted_iota(jnp.int32, (8, LANES), 0) == 0).astype(F32)
+        nsend[...] = jnp.zeros_like(nsend)
+        rrecv[0] = sums * (1.0 / width)
+        for k in range(half_heads - 1):
+            to_lane(k).wait_recv()
+
+        def finish_rows(c, _):
+            at_rows = rows_of(c)
+            grad = cown[half_heads - 1, at_rows].astype(F32)
+            for k in range(half_heads - 1):
+                grad = grad + yrecv[k, at_rows].astype(F32)
+            scale = rstd_r[at_rows]
+            hat = mine_r[at_rows].astype(F32) * scale
+            mean = dot(rrecv[0, :, at_rows], pick, TN, precision=HIGH)
+            nsend[0:1] += jnp.sum(grad * hat, axis=0, keepdims=True)
+            inside = pl.ds(pl.multiple_of(lax.rem(c, per) * chunk, chunk), chunk)
+            for q in range(share // LANES):
+                at = slice(q * LANES, (q + 1) * LANES)
+                up[c // per, inside, at] = (
+                    scale * (grad[:, at] * gain[:, at] - hat[:, at] * mean)
+                ).astype(BF16)
+            return 0
+
+        lax.fori_loop(0, head_size, finish_rows, 0)
+        for r in range(members):
+            @pl.when(r != member)
+            def _(r=r):
+                give(up, up_o, r, us_sem, ur_sem).start()
+
+        keep_up = pltpu.make_async_copy(up.at[member], up_o.at[member], copy_sem.at[1])
+        keep_up.start()
+
+        def share_norm(d):
+            return remote(nsend, nrecv.at[d - 1], ns_sem.at[d - 1], nr_sem.at[d - 1], seq_at(d), head)
+
+        for d in range(1, seq_size):
+            share_norm(d).start()
+
+        vectors_sum = vsend[...]
+        step_sum = tsend[place]
+        for d in range(1, seq_size):
+            vector(d).wait_recv()
+            vectors_sum = vectors_sum + vrecv[d - 1]
+            step_piece(d).wait_recv()
+            step_sum = step_sum + trecv[d - 1]
+        vec_o[...] = vectors_sum
+        step_o[...] = step_sum
+        for d in range(1, seq_size):
+            source = seq_at(d)
+            remote(sall.at[source], sall.at[source], sas_sem.at[d - 1], sar_sem.at[seq_size - 1 - d],
+                   seq, head).wait_recv()
+        state_o[...] = sall[...].astype(F32)
+
+        def settle(out, own, copy, landed):
+            def one(k, total):
+                copy(k).wait_recv()
+                return total + landed[k].astype(F32)
+
+            out[...] = lax.fori_loop(0, outer - 1, one, own.astype(F32))
+
+        load_half.wait()
+        settle(gate_o, gown[...], along_gate, grecv)
+        norm = nsend[...]
+        for d in range(1, seq_size):
+            share_norm(d).wait_recv()
+            norm = norm + nrecv[d - 1]
+        norm_o[...] = norm
+        settle(value_o, duo[outer - 1, side], along, zrecv)
+
+        for r in range(members):
+            @pl.when(r != member)
+            def _(r=r):
+                remote(up.at[r], up_o.at[r], us_sem.at[r], ur_sem.at[r], base + r, head).wait()
+                remote(branch_rows(r), branch_o.at[r], bs_sem.at[r], br_sem.at[r], base + r, head).wait()
+
+            @pl.when(r == member)
+            def _(r=r):
+                pltpu.make_async_copy(branch_rows(r), branch_o.at[r], copy_sem.at[0]).wait()
+
+        keep_up.wait()
+
+        def drain(k, _):
+            cross(k).wait_send()
+            return 0
+
+        def drain_along(k, _):
+            along(k).wait_send()
+            along_gate(k).wait_send()
+            return 0
+
+        lax.fori_loop(0, outer, drain, 0)
+        lax.fori_loop(0, outer - 1, drain_along, 0)
+        for k in range(half_heads):
+            to_core(k).wait_send()
+            if k < half_heads - 1:
+                to_lane(k).wait_send()
+
+        @pl.when(group > 0)
+        def _():
+            edge_back(head_r, hrecv, h_sem).wait_send()
+            edge_back(low.at[pl.ds(0, EDGE)], hbrecv, hb_sem).wait_send()
+
+        for k in range(half_heads):
+            part_core(k).wait_send()
+            if k < half_heads - 1:
+                part_lane(k).wait_send()
+        for d in range(1, head_size):
+            row_sums(d).wait_send()
+            basis_sum(d).wait_send()
+        for d in range(1, seq_size):
+            share_norm(d).wait_send()
+            vector(d).wait_send()
+            step_piece(d).wait_send()
+            state_piece(d).wait_send()
+            state_share(d).wait_send()
+
+    vmem = pl.BlockSpec(memory_space=pltpu.VMEM)
+    anywhere = pl.BlockSpec(memory_space=pl.ANY)
+    dma = pltpu.SemaphoreType.DMA
+    args = (normal_in, dz, dxr, tail, head_rows, gate_matrix, value_matrix, state_matrix, step_matrix,
+            value_kernel, state_kernel, state_bias, state_pre, state_edge, dbc, ddtr, vectors, small,
+            part, mine, rstd, gain_share, gate_half)
+    far = {2, 5, 6, 12, 14, 18, 22}
+    moves = lambda *dims: pltpu.VMEM(dims, BF16)
+    plain = lambda *dims: pltpu.VMEM(dims, F32)
+    return pl.pallas_call(
+        kernel,
+        in_specs=[anywhere if i in far else vmem for i in range(len(args))],
+        out_specs=[vmem] * 6 + [anywhere, anywhere],
+        out_shape=[
+            shape((strip, channels), F32), shape((strip, channels), F32),
+            shape((seq_size, piece, both), F32), shape((heads, 2 * strip), F32),
+            shape((8, packed), F32), shape((8, share), F32),
+            shape((members, length, share), BF16), shape((members, length, share), BF16),
+        ],
+        scratch_shapes=[
+            moves(rows, channels), moves(outer, 2, strip, channels), moves(outer, strip, channels),
+            moves(outer - 1, strip, channels), moves(strip, channels),
+            moves(outer - 1, strip, channels), moves(2, 2, share, channels), plain(rows, LANES),
+            moves(half_heads, rows, share), moves(half_heads, rows, share),
+            moves(half_heads, rows, share), moves(half_heads - 1, rows, share),
+            plain(8, rows), plain(head_size - 1, 8, rows), moves(members, length, share),
+            plain(8, share), plain(seq_size - 1, 8, share),
+            moves(half_heads, rows, share), moves(half_heads, rows, share),
+            moves(half_heads - 1, rows, share),
+            plain(head_size - 1, chunk, both), plain(rows, both), plain(2 * EDGE, channels),
+            plain(EDGE, channels), plain(EDGE, both), plain(rows + EDGE, both),
+            pltpu.VMEM((seq_size, piece, both), piece_type),
+            pltpu.VMEM((seq_size - 1, piece, both), piece_type),
+            plain(8, LANES),
+            pltpu.VMEM((seq_size, piece, both), piece_type),
+            plain(outer, heads, 2 * strip), plain(seq_size - 1, heads, 2 * strip),
+            plain(8, packed), plain(seq_size - 1, 8, packed),
+            dma((outer,)), dma((outer,)), dma((outer - 1,)), dma((outer - 1,)),
+            dma((half_heads,)), dma((half_heads,)), dma((half_heads - 1,)), dma((half_heads - 1,)),
+            dma((head_size - 1,)), dma((head_size - 1,)),
+            dma((members,)), dma((members,)), dma((seq_size - 1,)), dma((seq_size - 1,)),
+            dma((half_heads,)), dma((half_heads,)), dma((half_heads - 1,)), dma((half_heads - 1,)),
+            dma((head_size - 1,)), dma((head_size - 1,)), dma((head_size - 1,)), dma((head_size - 1,)),
+            dma((2,)), dma((2,)),
+            dma((seq_size - 1,)), dma((seq_size - 1,)), dma((seq_size - 1,)), dma((seq_size - 1,)),
+            dma((seq_size - 1,)), dma((seq_size - 1,)), dma((seq_size - 1,)), dma((seq_size - 1,)),
+            dma((members,)), dma((members,)), dma((outer - 1,)), dma((outer - 1,)), dma((2, 2)),
+            dma((4 + half_heads,)),
+        ],
+        compiler_params=pltpu.CompilerParams(
+            collective_id=1, has_side_effects=True, vmem_limit_bytes=VMEM_BYTES
+        ),
+        cost_estimate=pl.CostEstimate(
+            flops=60_000_000_000, bytes_accessed=300_000_000, transcendentals=0
+        ),
+        name="closing_sums",
+    )(*args)
+
 def shifted(block, axis, distance):
     devices = range(lax.axis_size(axis))
     route = [(i - distance, i) for i in devices if i - distance in devices]
@@ -547,25 +1132,6 @@
         leaving = decay * carry.astype(F32) + part.astype(F32)
         carry = shifted(leaving.astype(BF16), "seq", distance)
     return carry
-
-
-def depthwise(padded, kernel, offset, length):
-    summed = offset + kernel[0] * padded[0:length]
-    for tap_index in range(1, kernel.shape[0]):
-        summed = summed + kernel[tap_index] * padded[tap_index : tap_index + length]
-    return summed
-
-
-def depthwise_back(extended, kernel, length):
-    margin = kernel.shape[0] - 1
-    summed = kernel[0] * extended[margin : margin + length]
-    for k in range(1, kernel.shape[0]):
-        summed = summed + kernel[k] * extended[margin - k : margin - k + length]
-    return summed
-
-
-def kernel_sums(padded, pre_grad, length, taps):
-    return jnp.stack([jnp.sum(pre_grad * padded[k : k + length], axis=0) for k in range(taps)])
 
 
 def summed_low(part, dim):
@@ -601,10 +1167,11 @@
     rows = seq_count * length
     head_count = lax.axis_size("head")
     head_rank = lax.axis_index("head")
-    inner = channels * head_count
     row = lambda v: v.reshape(1, -1)
 
-    whole_in = lax.all_gather(regroup(tokens), "head", axis=2, tiled=True).reshape(rows, width)
+    mine = regroup(tokens)
+    whole_in = lax.all_gather(mine, "head", axis=2, tiled=True).reshape(rows, width)
+    mine = mine.reshape(rows, share)
     flat_cot = lax.all_gather(regroup(cotangent), "head", axis=2, tiled=True).reshape(rows, width)
     plain = whole_in.astype(F32)
     rstd = lax.rsqrt(jnp.mean(plain * plain, axis=-1, keepdims=True) + EPSILON)
@@ -632,102 +1199,55 @@
     )
     sums = lax.psum(sums, "head")
     normed, part, dy, dz, dv, ab, ds0, post, starting, gate_gain_part = turn(
-        y, gate_pre, normed_grad, xs, bcs, cum, sums, row(gate_gain), output_matrix, dec, length, inner
+        y, gate_pre, normed_grad, xs, bcs, cum, sums, row(gate_gain), output_matrix, dec, length, head_count
     )
     back = carried(starting, whole_decay, hops, -seq_count)
-    branch = lax.psum_scatter(part, "head", scatter_dimension=1, tiled=True)
-    layer_out = (
-        tokens.astype(F32) + regroup(branch.reshape(tokens.shape)).astype(F32)
-    ).astype(BF16)
     output_partial = dot(normed, flat_cot, TN)
-    gate_partial = dot(normal_in, dz, TN)
+    seq_size = lax.axis_size("seq")
+    gate_keep, gate_give = halves(normal_in, dz, seq_size // 2)
+    gate_half = lax.ppermute(gate_give, "seq", [(i, i ^ 1) for i in range(seq_size)])
+    gate_half = (gate_keep.astype(F32) + gate_half.astype(F32)).astype(BF16)
     g, dbc_intra = intra_back(bcs, xdt, dy, cum, cumt, length)
     dxr, tail, head_rows, value_kernel_part, value_bias_part, ddtr, dbc, small = finish_back(
         value_pre, value_edge, value_kernel, row(value_bias), xs, xdt, xw, g, dy, dv, bcs, step_pre, dt, cum,
         ab, hin0, pre, carry, hin_low, ds0, post, back, dec, dbc_intra, skip_row, row(skip_gain),
         row(step_bias), row(log_rate), length,
     )
-    dbc = lax.psum(dbc, "head")
-    state_padded = jnp.concatenate([state_edge[EDGE - taps + 1 :], state_pre], axis=0)
-    state_conv = depthwise(state_padded, state_kernel, state_bias, rows)
-    dpre_bc = dbc * slope(state_conv)
-    after = shifted(jnp.concatenate([head_rows, dpre_bc[:EDGE]], axis=1), "seq", -seq_count)
-    value_after, state_after = after[:, :channels], after[:, channels:]
-    zeros = jnp.zeros_like(value_after)
-    fixed = tail + depthwise_back(
-        jnp.concatenate([zeros, value_after[: taps - 1]], axis=0), value_kernel, EDGE
-    )
-    dxr = lax.dynamic_update_slice(dxr, fixed.astype(BF16), (rows - EDGE, 0))
-    dbc_low = depthwise_back(
-        jnp.concatenate([dpre_bc, state_after[: taps - 1]], axis=0), state_kernel, rows
-    ).astype(BF16)
-    state_kernel_part = kernel_sums(state_padded, dpre_bc, rows, taps)
-    state_bias_part = jnp.sum(dpre_bc, axis=0)
-
-    column_share = both // head_count
-    state_columns = lax.dynamic_slice_in_dim(dbc_low, head_rank * column_share, column_share, 1)
-    matrix_columns = lax.dynamic_slice_in_dim(
-        state_matrix, head_rank * column_share, column_share, 1
-    )
-    value_partial = dot(normal_in, dxr, TN)
-    normal_partial = (
-        dot(dz, gate_matrix, NT)
-        + dot(dxr, value_matrix, NT)
-        + dot(state_columns, matrix_columns, NT)
-        + dot(ddtr, step_matrix, NT)
+    vectors = jnp.concatenate(
+        [value_kernel_part, value_bias_part, gate_gain_part, jnp.zeros((2, channels), F32)], axis=0
     )
     gain_share = lax.dynamic_slice_in_dim(norm_gain, head_rank * share, share, 0)
-    own_hat = lax.dynamic_slice_in_dim(plain, head_rank * share, share, 1) * rstd
-    row_total = lax.psum(
-        jnp.sum(normal_partial * norm_gain * (plain * rstd), axis=-1, keepdims=True), "head"
-    )
-    normal_grad = lax.psum_scatter(
-        normal_partial.astype(BF16), "head", scatter_dimension=1, tiled=True
-    ).astype(F32)
-    up = rstd * (normal_grad * gain_share - own_hat * row_total / width)
-    token_grad = cotangent.astype(F32) + regroup(up.astype(BF16).reshape(tokens.shape)).astype(F32)
-    norm_gain_part = jnp.sum(normal_grad * own_hat, axis=0)
-    step_partial = dot(normal_in, ddtr, TN)
-    own_rows = lax.dynamic_slice_in_dim(normal_in, head_rank * share, share, 1)
-    state_partial = dot(own_rows, dbc_low, TN)
-    gate_matrix_grad, value_matrix_grad, step_matrix_grad, output_matrix_grad = (
-        summed_low(gate_partial, 0),
-        summed_low(value_partial, 0),
-        lax.psum_scatter(step_partial, "seq", scatter_dimension=0, tiled=True),
-        summed_low(output_partial, 1),
-    )
-    summed = lax.psum(
-        (
-            state_partial,
-            norm_gain_part,
-            value_kernel_part,
-            value_bias_part[0],
-            state_kernel_part,
-            state_bias_part,
-            small[0],
-            small[1],
-            small[2],
-            gate_gain_part[0],
-        ),
-        "seq",
-    )
+    gate_grad, value_grad, state_grad, step_grad, sums_out, norm_grad, up, branch = closing(
+        normal_in, dz, dxr, tail, head_rows, gate_matrix, value_matrix, state_matrix, step_matrix,
+        value_kernel, state_kernel, row(state_bias), state_pre, state_edge, dbc, ddtr, vectors, small,
+        part, mine, rstd, row(gain_share), gate_half, length, seq_size, head_count,
+    )
+    token_grad = cotangent.astype(F32) + up.astype(F32)
+    layer_out = (tokens.astype(F32) + branch.astype(F32)).astype(BF16)
+    output_grad = summed_low(output_partial, 1)
+    strip = width // seq_size
+    step_grad = lax.dynamic_slice_in_dim(
+        step_grad, lax.rem(lax.axis_index("seq"), 2) * strip, strip, 1
+    ).T
+    state_sums = sums_out[:, channels : channels + both]
+    small_sums = sums_out[:, channels + both : channels + both + heads]
     return (
         layer_out,
         token_grad,
-        summed[1],
-        gate_matrix_grad,
-        value_matrix_grad,
-        summed[0],
-        step_matrix_grad,
-        summed[2],
-        summed[3],
-        summed[4],
-        summed[5],
-        summed[6],
-        summed[7],
-        summed[8],
-        summed[9],
-        output_matrix_grad,
+        norm_grad[0],
+        gate_grad,
+        value_grad,
+        state_grad.reshape(share, both),
+        step_grad,
+        sums_out[:taps, :channels],
+        sums_out[taps, :channels],
+        state_sums[:taps],
+        state_sums[taps],
+        small_sums[0],
+        small_sums[1],
+        small_sums[2],
+        sums_out[taps + 1, :channels],
+        output_grad,
     )
 
 

time: 781 us -> 450 us (0.58)
  waiting for transfers between devices: 422 us -> 33.3 us
  Pallas kernels: 88.8 us -> 264 us
  matrix products: 89.2 us -> 31.7 us
  blocking collectives: 99.4 us -> 55.5 us
  other arithmetic: 28 us -> 14.1 us
  starting transfers between devices: 18.8 us -> 10.3 us
    reduce_scatter x3 -> x1, waiting for transfers between devices: 265 us -> 0.01 us  [summed_low(): lax.psum_scatter(low, 'seq', scatter_dimension=dim, tiled=True).astype(F32)]
    pallas_call x0 -> x1, Pallas kernels: none -> 165 us  [closing(): pl.pallas_call(kernel, in_specs=[anywhere if i in far else vmem for i in...]
    psum x2 -> x0, waiting for transfers between devices: 109 us -> none  [the longest x1 75.2 us: local(): lax.psum((state_partial, norm_gain_part, value_kernel_part, value_bias_pa...]
    dot_general x14 -> x6, matrix products: 89.2 us -> 31.7 us  [dot(): lax.dot_general(a, b, dims, precision=precision, preferred_element_type=F32)]
    psum x2 -> x0, blocking collectives: 43.9 us -> none  [the longest x1 37.1 us: local(): lax.psum((state_partial, norm_gain_part, value_kernel_part, value_bias_pa...]
    reduce_scatter x3 -> x0, waiting for transfers between devices: 28.7 us -> none  [the longest x1 21.2 us: local(): lax.psum_scatter(step_partial, 'seq', scatter_dimension=0, tiled=True)]
    ppermute x4 -> x3, waiting for transfers between devices: 3.23 us -> 17.6 us  [shifted(): return lax.ppermute(block, axis, route)]
    pallas_call x6 -> x7, Pallas kernels: 88.8 us -> 98.7 us  [call(): pl.pallas_call(kernel, grid=grid, in_specs=in_specs, out_specs=out_specs,...]
  transfers between devices with their start and end apart: 16 -> 7, of which waited for: 9 -> 2; matrix products, arithmetic and copies ran while one was open for 16% -> 13% of each run, Pallas kernels for 4% -> 51%
where the time goes in v3:
time: 450 us; the launch traced here: 442 us
  Pallas kernels  264 us (59%)
  blocking collectives  55.5 us (12%)
  waiting for transfers between devices  33.3 us (7%)
  matrix products  31.7 us (7%)
  local copies, waits for them, and re-layouts  19.6 us (4%)
  between operations  14.2 us (3%)
  other arithmetic  14.1 us (3%)
  starting transfers between devices  10.3 us (2%)
    pallas_call x1, Pallas kernels, closing(): pl.pallas_call(kernel, in_specs=[anywhere if i in far else vmem for i in...  165 us
    pallas_call x7, Pallas kernels, call(): pl.pallas_call(kernel, grid=grid, in_specs=in_specs, out_specs=out_specs,...  98.7 us
    all_to_all x2, blocking collectives, regroup(): lax.all_to_all(block, 'seq', 0, 0, axis_index_groups=groups, tiled=True)  37.9 us
    dot_general x6, matrix products, dot(): lax.dot_general(a, b, dims, precision=precision, preferred_element_type=F32)  31.7 us
    ppermute x3, waiting for transfers between devices, shifted(): return lax.ppermute(block, axis, route)  17.6 us
    psum x1, blocking collectives, local(): sums = lax.psum(sums, 'head')  17.6 us
    all_gather x1, waiting for transfers between devices, local(): lax.all_gather(mine, 'head', axis=2, tiled=True).reshape(rows, width)  15.7 us
  transfers between devices with their start and end apart: 7, of which 2 were waited for; matrix products, arithmetic and copies ran while one was open for 13% of the time, Pallas kernels for 51%

profile of v3, /device:TPU:0, one launch (start us, length us, event | category | flops | bytes accessed | tf_op | source)
XLA Modules:
  0.0 442.4 jit_solution(3214777085767357036)
XLA Ops:
  7.2 20.1 %all_to_all.10 = bf16[4,256,512]{2,1,0:T(8,128)(2,1)} all-to-all(bf16[4,256,512]{2,1,0:T(8,128)(2,1)} %param.16), channel_id=1, replica_groups={{0,4,8,12},{16,20,24,28},{1,5,9,13},{17,21,25,29},{2,6,10,14},{18,22,26..., dimensions={0} | all-to-all | bytes 2097152 | tf_op jit(solution)/shard_map/all_to_all | solution.py:1126
  27.4 17.9 %all_to_all.11 = bf16[4,256,512]{2,1,0:T(8,128)(2,1)} all-to-all(bf16[4,256,512]{2,1,0:T(8,128)(2,1)} %param.17), channel_id=1, replica_groups={{0,4,8,12},{16,20,24,28},{1,5,9,13},{17,21,25,29},{2,6,10,14},{18,22,26..., dimensions={0} | all-to-all | bytes 2097152 | tf_op jit(solution)/shard_map/all_to_all | solution.py:1126
  46.1 15.7 %all-gather.3.cloned.1.call-done = bf16[4,256,2048]{2,1,0:T(8,128)(2,1)} async-done(((bf16[4,256,512]{2,1,0:T(8,128)(2,1)}), bf16[4,256,2048]{2,1,0:T(8,128)(2,1)}) %all-gather.3.cloned.1.call-update) | async-done | bytes 4194320 | tf_op jit(solution)/shard_map/all_gather | solution.py:1173
  61.8 3.2 multiply_reduce_fusion
  67.4 4.5 %fusion.5.xr.xr_before = f32[1024,1024]{1,0:T(8,128)S(1)} fusion(bf16[1024,2048]{1,0:T(8,128)(2,1)S(1)} %fusion.1.xn, bf16[2048,1024]{1,0:T(8,128)(2,1)S(1)} %copy-done.16), kind=kOutput, calls=%fused_computation.18 | convolution fusion | flops 4294967296 | bytes 12582912 | tf_op jit(solution)/shard_map/dot_general | solution.py:22
  73.3 4.8 %collective-permute-start = (f32[8,1280]{1,0:T(8,128)S(1)}, f32[8,1280]{1,0:T(8,128)S(1)}, u32[]{:S(2)}, u32[]{:S(2)}) collective-permute-start(f32[8,1280]{1,0:T(8,128)S(1)} %pad_maximum_fusion), channel_id=1, source_target_pairs={{0,16},{4,20},{8,24},{12,28},{1,17},{5,21},{9,25},{13,29},{2,18},{... | collective-permute-start | bytes 122888 | tf_op jit(solution)/shard_map/ppermute | solution.py:1119
  78.1 6.1 %fusion.8.z.z_r = f32[1024,1024]{1,0:T(8,128)} fusion(bf16[1024,2048]{1,0:T(8,128)(2,1)S(1)} %fusion.1.xn, bf16[2048,1024]{1,0:T(8,128)(2,1)S(1)} %copy-done.17), kind=kOutput, calls=%fused_computation.21 | convolution fusion | flops 4294967296 | bytes 12582912 | tf_op jit(solution)/shard_map/dot_general | solution.py:22
  84.2 2.0 fusion.7.dtr
  87.4 15.7 %conv_and_local_states.1 = (bf16[1024,1024]{1,0:T(8,128)(2,1)}, bf16[1024,1024]{1,0:T(8,128)(2,1)}, bf16[1024,1024]{1,0:T(8,128)(2,1)}, bf16[1024,256]{1,0:T(8,1...) custom-call(f32[1024,1024]{1,0:T(8,128)} %copy-done, ...), custom_call_target="tpu_custom_call" | custom-call | flops 268435456 | bytes 20055168 | tf_op jit(solution)/shard_map/conv_and_local_states/pallas_call | solution.py:74
  103.1 2.3 collective-permute-start.1
  105.4 10.0 %fusion.9.dn.dn_r = f32[1024,1024]{1,0:T(8,128)} fusion(bf16[1024,2048]{1,0:T(8,128)(2,1)} %bitcast.69, bf16[1024,2048]{1,0:T(8,128)(2,1)} %wo.1), kind=kOutput, calls=%fused_computation.22 | convolution fusion | flops 4294967296 | bytes 12582912 | tf_op jit(solution)/shard_map/dot_general | solution.py:22
  115.5 6.7 %within_blocks.1.yi = f32[1024,1024]{1,0:T(8,128)} custom-call(bf16[1024,256]{1,0:T(8,128)(2,1)} %get-tuple-element.60.bcs_r, bf16[1024,1024]{1,0:T(8,128)(2,1)} %get-tuple-element.61.xdt_r, f32[1024,16]{1,0:T(8,128)} %get-tuple-element.62.cum_r, f32[16,1024]{1,0:T(8,128)} %get-tuple-element.63.cumt_r), custom_call_target="tpu_custom_call" | custom-call | flops 2147483648 | bytes 6946816 | tf_op jit(solution)/shard_map/within_blocks/pallas_call | solution.py:74
  122.9 10.3 %across_blocks.1 = (f32[1024,1024]{1,0:T(8,128)}, bf16[4,1024,128]{2,1,0:T(8,128)(2,1)}, f32[1024,2]{1,0:T(8,128)}) custom-call(f32[1024,1024]{1,0:T(8,128)} %within_blocks.1.yi, bf16[1024,1024]{1,0:T(8,128)(2,1)} %get-tuple-element.64.xs_r, bf16[1024,256]{1,0:T(8,128)(2,1)} %get-tuple-element.60.bcs_r, f32[1024,1024]{1,0:T(8,128)} %fusion.8.z.z_r, ...), custom_call_target="tpu_custom_call" | custom-call | flops 268435456 | bytes 22921216 | tf_op jit(solution)/shard_map/across_blocks/pallas_call | solution.py:74
  133.2 17.6 %psum.7.sums_r = f32[1024,2]{1,0:T(8,128)} all-reduce(f32[1024,2]{1,0:T(8,128)} %get-tuple-element.69), channel_id=1, replica_groups=mesh['seq'=8,'head'=4] {'head'}, use_global_device_ids=true, to_apply=%region_1.0 | all-reduce | flops 2048 | bytes 16384 | tf_op jit(solution)/shard_map/psum | solution.py:1200
  150.7 18.9 %gate_and_turn.1 = (bf16[1024,1024]{1,0:T(8,128)(2,1)}, bf16[4,1024,512]{2,1,0:T(8,128)(2,1)}, bf16[1024,1024]{1,0:T(8,128)(2,1)}, bf16[1024,1024]{1,0:T(8,128)(...) custom-call(f32[1024,1024]{1,0:T(8,128)} %get-tuple-element.68.y_r, ...), custom_call_target="tpu_custom_call" | custom-call | flops 4563402752 | bytes 34619392 | tf_op jit(solution)/shard_map/gate_and_turn/pallas_call | solution.py:74
  169.6 8.9 %gate_strips.1 = (bf16[4,256,1024]{2,1,0:T(8,128)(2,1)}, bf16[4,256,1024]{2,1,0:T(8,128)(2,1)}) custom-call(bf16[1024,2048]{1,0:T(8,128)(2,1)} %copy-done.5, bf16[1024,1024]{1,0:T(8,128)(2,1)} %get-tuple-element.71.grad_r.dz_r), custom_call_target="tpu_custom_call" | custom-call | flops 4294967296 | bytes 10485760 | tf_op jit(solution)/shard_map/gate_strips/pallas_call | solution.py:74
  180.0 7.8 %convolution_convert_fusion = bf16[1024,2048]{1,0:T(8,128)(2,1)} fusion(bf16[1024,1024]{1,0:T(8,128)(2,1)} %get-tuple-element.103, bf16[1024,2048]{1,0:T(8,128)(2,1)S(1)} %bitcast.70), kind=kOutput, calls=%fused_computation.5 | convolution fusion | flops 4297064448 | bytes 10485760 | tf_op jit(solution)/shard_map/dot_general | solution.py:22
  192.3 12.6 %within_blocks_back.1 = (f32[1024,1024]{1,0:T(8,128)}, f32[1024,256]{1,0:T(8,128)}) custom-call(bf16[1024,256]{1,0:T(8,128)(2,1)} %get-tuple-element.60.bcs_r, bf16[1024,1024]{1,0:T(8,128)(2,1)} %get-tuple-element.61.xdt_r, bf16[1024,1024]{1,0:T(8,128)(2,1)} %get-tuple-element.73.dy_r, f32[1024,16]{1,0:T(8,128)} %get-tuple-element.62.cum_r, ...), custom_call_target="tpu_custom_call" | custom-call | flops 4294967296 | bytes 10092544 | tf_op jit(solution)/shard_map/within_blocks_back/pallas_call | solution.py:74
  204.9 17.6 %collective-permute-done.2.back_r = bf16[1024,128]{1,0:T(8,128)(2,1)S(1)} collective-permute-done((bf16[1024,128]{1,0:T(8,128)(2,1)S(1)}, bf16[1024,128]{1,0:T(8,128)(2,1)S(1)}, u32[]{:S(2)}, u32[]{:S(2)}) %collective-permute-start.2) | collective-permute-done | bytes 262176 | tf_op jit(solution)/shard_map/ppermute | solution.py:1119
  223.2 25.6 %across_blocks_back.1 = (bf16[1024,1024]{1,0:T(8,128)(2,1)}, f32[8,1024]{1,0:T(8,128)}, f32[8,1024]{1,0:T(8,128)}, f32[4,1024]{1,0:T(4,128)}, f32[1,1024]{1,0:T(...) custom-call(f32[1024,1024]{1,0:T(8,128)} %copy-done, f32[1024,1024]{1,0:T(8,128)} %copy-done, ...), custom_call_target="tpu_custom_call" | custom-call | flops 805306368 | bytes 34157248 | tf_op jit(solution)/shard_map/across_blocks_back/pallas_call | solution.py:74
  250.3 2.3 add_convert_fusion.half_h
  252.6 164.9 %closing_sums.1 = (f32[256,1024]{1,0:T(8,128)}, f32[256,1024]{1,0:T(8,128)}, f32[8,64,256]{2,1,0:T(8,128)}, f32[16,512]{1,0:T(8,128)}, f32[8,1408]{1,0:T(8,128)}...) custom-call(bf16[1024,2048]{1,0:T(8,128)(2,1)} %copy-done.5, ...), custom_call_target="tpu_custom_call" | custom-call | flops 60000002048 | bytes 300000000 | tf_op jit(solution)/shard_map/closing_sums/pallas_call | solution.py:1067
  426.8 4.0 convert_add_fusion
  430.8 2.1 convert_element_type.55
  (83 shorter events, 26.7 us)
Async XLA Ops:
  7.2 38.1 %copy-start.15 = (f32[16]{0:T(128)S(1)}, f32[16]{0:T(128)}, u32[]{:S(2)}) copy-start(f32[16]{0:T(128)} %param.29) | copy-start | bytes 196
  7.2 54.6 %all-gather.3.cloned.1.call-start = ((), (), s32[]{:S(2)}) async-start(), calls=%async_computation.3 | async-start | bytes 5242880 | tf_op jit(solution)/shard_map/all_gather | solution.py:1173
  27.3 37.7 %copy-start.13 = (f32[2048]{0:T(1024)S(1)}, f32[2048]{0:T(1024)}, u32[]{:S(2)}) copy-start(f32[2048]{0:T(1024)} %param.18) | copy-start | bytes 24580
  27.3 78.1 %all-gather.5.cloned.1.call-start = ((), (), s32[]{:S(2)}) async-start(), calls=%async_computation.4 | async-start | bytes 5242880 | tf_op jit(solution)/shard_map/all_gather | solution.py:1175
  45.3 385.5 %reduce-scatter.2.cloned.1.call-start = ((), (), s32[]{:S(2)}) async-start(), calls=%async_computation.5 | async-start | bytes 4718592 | tf_op jit(solution)/shard_map/reduce_scatter | solution.py:1139
  61.8 3.4 copy-start.1
  67.4 16.8 %copy-start.5 = (bf16[1024,2048]{1,0:T(8,128)(2,1)}, bf16[1024,2048]{1,0:T(8,128)(2,1)S(1)}, u32[]{:S(2)}) copy-start(bf16[1024,2048]{1,0:T(8,128)(2,1)S(1)} %fusion.1.xn) | copy-start | bytes 12582916
  67.4 4.6 %copy-start.19 = (bf16[2048,256]{1,0:T(8,128)(2,1)S(1)}, bf16[2048,256]{1,0:T(8,128)(2,1)}, u32[]{:S(2)}) copy-start(bf16[2048,256]{1,0:T(8,128)(2,1)} %state_m.1) | copy-start | bytes 3145732
  71.9 12.2 %copy-start = (f32[1024,1024]{1,0:T(8,128)}, f32[1024,1024]{1,0:T(8,128)S(1)}, u32[]{:S(2)}) copy-start(f32[1024,1024]{1,0:T(8,128)S(1)} %fusion.5.xr.xr_before) | copy-start | bytes 12582916
  72.0 6.1 %copy-start.17 = (bf16[2048,1024]{1,0:T(8,128)(2,1)S(1)}, bf16[2048,1024]{1,0:T(8,128)(2,1)}, u32[]{:S(2)}) copy-start(bf16[2048,1024]{1,0:T(8,128)(2,1)} %gate_h.1) | copy-start | bytes 12582916
  73.3 10.9 %copy-start.2 = (f32[1024,256]{1,0:T(8,128)}, f32[1024,256]{1,0:T(8,128)S(1)}, u32[]{:S(2)}) copy-start(f32[1024,256]{1,0:T(8,128)S(1)} %fusion.6.bc.bc_before.bc_h) | copy-start | bytes 3145732
  73.3 10.9 %copy-start.12 = (bf16[2048,16]{0,1:T(8,128)(2,1)S(1)}, bf16[2048,16]{0,1:T(8,128)(2,1)}, u32[]{:S(2)}) copy-start(bf16[2048,16]{0,1:T(8,128)(2,1)} %param.22) | copy-start | bytes 196612
  73.3 12.9 %collective-permute-start = (f32[8,1280]{1,0:T(8,128)S(1)}, f32[8,1280]{1,0:T(8,128)S(1)}, u32[]{:S(2)}, u32[]{:S(2)}) collective-permute-start(f32[8,1280]{1,0:T(8,128)S(1)} %pad_maximum_fusion), channel_id=1, source_target_pairs={{0,16},{4,20},{8,24},{12,28},{1,17},{5,21},{9,25},{13,29},{2,18},{... | collective-permute-start | bytes 122888 | tf_op jit(solution)/shard_map/ppermute | solution.py:1119
  103.1 19.1 %collective-permute-start.1 = (bf16[1024,128]{1,0:T(8,128)(2,1)}, bf16[1024,128]{1,0:T(8,128)(2,1)S(1)}, u32[]{:S(2)}, u32[]{:S(2)}) collective-permute-start(bf16[1024,128]{1,0:T(8,128)(2,1)} %get-tuple-element.67), channel_id=1, source_target_pairs={{0,16},{4,20},{8,24},{12,28},{1,17},{5,21},{9,25},{13,29},{2,18},{... | collective-permute-start | bytes 786440 | tf_op jit(solution)/shard_map/ppermute | solution.py:1119
  169.6 10.4 %copy-start.18 = (bf16[4,256,2048]{2,1,0:T(8,128)(2,1)S(1)}, bf16[4,256,2048]{2,1,0:T(8,128)(2,1)}, u32[]{:S(2)}) copy-start(bf16[4,256,2048]{2,1,0:T(8,128)(2,1)} %all-gather.5.cloned.1.call-done) | copy-start | bytes 12582916
  178.5 71.7 %collective-permute-start.3 = (bf16[4,256,1024]{2,1,0:T(8,128)(2,1)}, bf16[4,256,1024]{2,1,0:T(8,128)(2,1)S(1)}, u32[]{:S(2)}, u32[]{:S(2)}) collective-permute-start(bf16[4,256,1024]{2,1,0:T(8,128)(2,1)} %get-tuple-element.94), channel_id=1, source_target_pairs={{0,4},{4,0},{8,12},{12,8},{16,20},{20,16},{24,28},{28,24},{1,5},{5... | collective-permute-start | bytes 6291464 | tf_op jit(solution)/shard_map/ppermute | solution.py:1208
  190.6 31.9 %collective-permute-start.2 = (bf16[1024,128]{1,0:T(8,128)(2,1)S(1)}, bf16[1024,128]{1,0:T(8,128)(2,1)S(1)}, u32[]{:S(2)}, u32[]{:S(2)}) collective-permute-start(bf16[1024,128]{1,0:T(8,128)(2,1)S(1)} %copy-done.20), channel_id=1, source_target_pairs={{16,0},{20,4},{24,8},{28,12},{17,1},{21,5},{25,9},{29,13},{18,2},{... | collective-permute-start | bytes 786440 | tf_op jit(solution)/shard_map/ppermute | solution.py:1119
  223.2 25.7 %copy-start.14 = (f32[1,1024]{1,0:T(1,128)S(1)}, f32[1,1024]{1,0:T(1,128)}, u32[]{:S(2)}) copy-start(f32[1,1024]{1,0:T(1,128)} %get-tuple-element.90) | copy-start | bytes 12292
  223.2 27.1 %copy-start.6 = (bf16[4,256,1024]{2,1,0:T(8,128)(2,1)S(1)}, bf16[4,256,1024]{2,1,0:T(8,128)(2,1)}, u32[]{:S(2)}) copy-start(bf16[4,256,1024]{2,1,0:T(8,128)(2,1)} %get-tuple-element.93) | copy-start | bytes 6291460
  252.6 174.2 %copy-start.3 = (bf16[4,256,512]{2,1,0:T(8,128)(2,1)S(1)}, bf16[4,256,512]{2,1,0:T(8,128)(2,1)}, u32[]{:S(2)}) copy-start(bf16[4,256,512]{2,1,0:T(8,128)(2,1)} %param.16) | copy-start | bytes 3145732
  252.6 174.2 %copy-start.4 = (bf16[4,256,512]{2,1,0:T(8,128)(2,1)S(1)}, bf16[4,256,512]{2,1,0:T(8,128)(2,1)}, u32[]{:S(2)}) copy-start(bf16[4,256,512]{2,1,0:T(8,128)(2,1)} %param.17) | copy-start | bytes 3145732
  426.8 6.2 %copy-start.9 = (f32[256,1024]{1,0:T(8,128)S(1)}, f32[256,1024]{1,0:T(8,128)}, u32[]{:S(2)}) copy-start(f32[256,1024]{1,0:T(8,128)} %get-tuple-element.132) | copy-start | bytes 3145732
  426.8 7.1 %copy-start.8 = (f32[256,1024]{1,0:T(8,128)S(1)}, f32[256,1024]{1,0:T(8,128)}, u32[]{:S(2)}) copy-start(f32[256,1024]{1,0:T(8,128)} %get-tuple-element.133) | copy-start | bytes 3145732
  430.8 4.1 copy-start.10
  (4 other events, 6.4 us)
Sparse Core Ops, SparseCore 0:
  27.5 34.2 all-gather.2
  63.3 34.4 all-gather.4
  188.0 131.4 reduce-scatter.1
